TPU v7x, 32 devices: a whole 2x2x4 slice. The times are simulated.
32 devices in a mesh: dp: 8 (over y, x, core), chan: 4 (over z).
Axes of the slice: x: 2, y: 2, z: 4, core: 2. Of those that a mesh axis runs over, the one named last changes fastest.
Arguments:
- spectra: bfloat16 [16, 256, 3072], P('dp', 'chan'), may hold values from -6 to 6
- lengths: int32 [16], P('dp'), may hold values from 25 to 384, as said below
- weight_in: bfloat16 [9, 512, 256], P(None, 'chan'), may hold values from -0.125 to 0.125
- gamma_in: float32 [512], P('chan'), may hold values from 0.5 to 2
- beta_in: float32 [512], P('chan'), may hold values from -2 to 2
- weight_mid: bfloat16 [9, 512, 512], P(None, 'chan'), may hold values from -0.09375 to 0.09375
- gamma_mid: float32 [512], P('chan'), may hold values from 0.5 to 2
- beta_mid: float32 [512], P('chan'), may hold values from -2 to 2
- cotangent: bfloat16 [16, 512, 768], P('dp', 'chan'), may hold values from -6 to 6
Outputs:
- block_out: bfloat16 [16, 512, 768], P('dp', 'chan')
- spectra_grad: float32 [16, 256, 3072], P('dp', 'chan')
- weight_in_grad: float32 [9, 512, 256], P(None, 'chan')
- gamma_in_grad: float32 [512], P('chan')
- beta_in_grad: float32 [512], P('chan')
- weight_mid_grad: float32 [9, 512, 512], P(None, 'chan')
- gamma_mid_grad: float32 [512], P('chan')
- beta_mid_grad: float32 [512], P('chan')
- root_squares: float32 [4], replicated
Inputs may be any that keep to these rules, and one draw needn't show every extreme that they name: `lengths`: some clip has exactly 384 valid frames.
All inputs are finite; a program needn't handle non-finite values.
Results may differ from a plain program's by a relative error of at most 0.014.
Values may be sent and summed in bfloat16 or wider, within the bound.
No kernel may reach another device: no remote copies, remote signals or barrier semaphores. Data moves between devices by JAX's collectives and lax.ppermute only.
A program may use at most 256 MiB of HBM per device.

v0:
```python
import jax
import jax.numpy as jnp
from jax import lax
from jax.sharding import PartitionSpec as P

C_IN = 256
C_MID = 512
MEL = 8


def shifted(field, tap):
    along = tap // 3 - 1
    across = tap % 3 - 1
    extent = field.shape[2]
    margin = MEL + 1
    padded = jnp.pad(field, ((0, 0), (0, 0), (margin, margin)))
    offset = margin + along * MEL + across
    moved = lax.slice_in_dim(padded, offset, offset + extent, axis=2)
    column = jnp.arange(extent, dtype=jnp.int32) % MEL + across
    inside = (column >= 0) & (column < MEL)
    return jnp.where(inside[None, None, :], moved, jnp.zeros_like(moved))


def convolve(field, weight):
    total = None
    for tap in range(9):
        term = jnp.einsum(
            "oi,nip->nop", weight[tap], shifted(field, tap), preferred_element_type=jnp.float32
        )
        total = term if total is None else total + term
    return total


def convolve_back(grads, weight):
    total = None
    for tap in range(9):
        term = jnp.einsum(
            "oi,nop->nip", weight[tap], shifted(grads, 8 - tap), preferred_element_type=jnp.float32
        )
        total = term if total is None else total + term
    return total


def weight_terms(grads, field):
    return jnp.stack(
        [
            jnp.einsum(
                "nop,nip->oi", grads, shifted(field, tap), preferred_element_type=jnp.float32
            )
            for tap in range(9)
        ]
    )


def local_sums(pre, mask):
    return (jnp.sum(pre * mask, axis=(0, 2)), jnp.sum(pre * pre * mask, axis=(0, 2)))


def norm_forward(pre, mask, first_total, second_total, count, gamma, beta):
    mean = first_total / count
    inverse = lax.rsqrt(second_total / count - mean * mean + 1e-05)
    scaled = (pre - mean[None, :, None]) * inverse[None, :, None]
    affine = gamma[None, :, None] * scaled + beta[None, :, None]
    return (jax.nn.silu(affine) * mask, scaled, affine, inverse)


def norm_local(grad_act, mask, scaled, affine):
    sigma = jax.nn.sigmoid(affine)
    local = grad_act * mask * sigma * (1.0 + affine * (1.0 - sigma))
    return (local, jnp.sum(local, axis=(0, 2)), jnp.sum(local * scaled, axis=(0, 2)))


def norm_back(local, scaled, inverse, gamma, mask, count, beta_grad, gamma_grad):
    factor = (gamma * inverse)[None, :, None]
    return (
        mask
        * factor
        * (local - beta_grad[None, :, None] / count - scaled * gamma_grad[None, :, None] / count)
    )


def pool_pairs(field):
    pairs = field[..., 0::2] + field[..., 1::2]
    rows = pairs.reshape(pairs.shape[0], pairs.shape[1], -1, MEL)
    return (rows[..., : MEL // 2] + rows[..., MEL // 2 :]).reshape(
        pairs.shape[0], pairs.shape[1], -1
    )


def spread_pairs(field):
    clips, channels = (field.shape[0], field.shape[1])
    grid = field.reshape(clips, channels, -1, 1, MEL // 2, 1)
    wide = jnp.broadcast_to(grid, (clips, channels, grid.shape[2], 2, MEL // 2, 2))
    return wide.reshape(clips, channels, -1)


def body(
    spectra, lengths, weight_in, gamma_in, beta_in, weight_mid, gamma_mid, beta_mid, cotangent
):
    extent = spectra.shape[2]
    frames = jnp.arange(extent, dtype=jnp.int32) // MEL
    mask = (frames[None, :] < lengths[:, None]).astype(jnp.float32)[:, None, :]
    starts = 2 * jnp.arange(extent // (2 * MEL), dtype=jnp.int32)
    inside = jnp.clip(lengths[:, None] - starts[None, :], 0, 2)
    divisor = 2.0 * jnp.maximum(inside, 1).astype(jnp.float32)
    pooled_div = jnp.repeat(divisor, MEL // 2, axis=1)[:, None, :]
    masked = spectra * mask.astype(jnp.bfloat16)
    gathered_in = lax.all_gather(masked, "chan", axis=1, tiled=True)
    first_pre = convolve(gathered_in, weight_in)
    first_one, first_two = local_sums(first_pre, mask)
    first_one, first_two, frame_total, pair_total = lax.psum(
        (
            first_one,
            first_two,
            jnp.sum(lengths).astype(jnp.float32),
            jnp.sum((lengths + 1) // 2).astype(jnp.float32),
        ),
        "dp",
    )
    count = MEL * frame_total
    pooled_count = MEL // 2 * pair_total
    first_act, first_scaled, first_affine, first_inverse = norm_forward(
        first_pre, mask, first_one, first_two, count, gamma_in, beta_in
    )
    gathered_mid = lax.all_gather(first_act.astype(jnp.bfloat16), "chan", axis=1, tiled=True)
    second_pre = convolve(gathered_mid, weight_mid)
    second_one, second_two = local_sums(second_pre, mask)
    second_one, second_two = lax.psum((second_one, second_two), "dp")
    second_act, second_scaled, second_affine, second_inverse = norm_forward(
        second_pre, mask, second_one, second_two, count, gamma_mid, beta_mid
    )
    pooled = pool_pairs(second_act) / pooled_div
    masked_wide = masked.astype(jnp.float32)
    totals = lax.psum(
        (
            jnp.sum(masked_wide * masked_wide),
            jnp.sum(first_act * first_act),
            jnp.sum(second_act * second_act),
            jnp.sum(pooled * pooled),
        ),
        ("dp", "chan"),
    )
    denominators = jnp.stack([count * C_IN, count * C_MID, count * C_MID, pooled_count * C_MID])
    root_squares = jnp.sqrt(jnp.stack(totals) / denominators)
    act_grad = spread_pairs(cotangent.astype(jnp.float32) / pooled_div)
    second_local, second_beta, second_gamma = norm_local(
        act_grad, mask, second_scaled, second_affine
    )
    beta_mid_grad, gamma_mid_grad = lax.psum((second_beta, second_gamma), "dp")
    second_grad = norm_back(
        second_local,
        second_scaled,
        second_inverse,
        gamma_mid,
        mask,
        count,
        beta_mid_grad,
        gamma_mid_grad,
    ).astype(jnp.bfloat16)
    weight_mid_local = weight_terms(second_grad, gathered_mid)
    weight_mid_grad = lax.psum(weight_mid_local.astype(jnp.bfloat16), "dp").astype(jnp.float32)
    mid_grad = lax.psum_scatter(
        convolve_back(second_grad, weight_mid), "chan", scatter_dimension=1, tiled=True
    )
    first_local, first_beta, first_gamma = norm_local(mid_grad, mask, first_scaled, first_affine)
    beta_in_grad, gamma_in_grad = lax.psum((first_beta, first_gamma), "dp")
    first_grad = norm_back(
        first_local, first_scaled, first_inverse, gamma_in, mask, count, beta_in_grad, gamma_in_grad
    ).astype(jnp.bfloat16)
    weight_in_local = weight_terms(first_grad, gathered_in)
    spectra_part = lax.psum_scatter(
        convolve_back(first_grad, weight_in).astype(jnp.bfloat16),
        "chan",
        scatter_dimension=1,
        tiled=True,
    ).astype(jnp.float32)
    spectra_grad = spectra_part * mask
    weight_in_grad = lax.psum(weight_in_local.astype(jnp.bfloat16), "dp").astype(jnp.float32)
    block_out = pooled.astype(jnp.bfloat16)
    return (
        block_out,
        spectra_grad,
        weight_in_grad,
        gamma_in_grad,
        beta_in_grad,
        weight_mid_grad,
        gamma_mid_grad,
        beta_mid_grad,
        root_squares,
    )


def solution(mesh):
    placed = (
        P("dp", "chan", None),
        P("dp"),
        P(None, "chan", None),
        P("chan"),
        P("chan"),
        P(None, "chan", None),
        P("chan"),
        P("chan"),
        P("dp", "chan", None),
    )
    return jax.shard_map(
        body,
        mesh=mesh,
        in_specs=placed,
        out_specs=(
            P("dp", "chan", None),
            P("dp", "chan", None),
            P(None, "chan", None),
            P("chan"),
            P("chan"),
            P(None, "chan", None),
            P("chan"),
            P("chan"),
            P(),
        ),
        check_vma=False,
    )
```

profile of v0, /device:TPU:0, one launch (start us, length us, event | category | flops | bytes accessed | tf_op | source)
XLA Modules:
  0.0 847.7 jit_solution(6448619360056174782)
XLA Ops:
  8.0 3.0 multiply_reduce_fusion.6
  13.0 64.3 %all-gather.3.cloned.1.call-done = bf16[2,256,3072]{2,1,0:T(8,128)(2,1)} async-done(((bf16[2,64,3072]{2,1,0:T(8,128)(2,1)}), bf16[2,256,3072]{2,1,0:T(8,128)(2,1)}) %all-gather.3.cloned.1.call-update) | async-done | bytes 3145744 | tf_op jit(solution)/shard_map/all_gather | solution.py:108
  77.3 4.9 fusion.16
  82.2 2.3 convolution_add_fusion.15
  84.5 2.3 convolution_add_fusion.14
  86.8 2.3 convolution_add_fusion.13
  90.2 2.5 convolution_add_fusion.11
  92.8 2.3 convolution_add_fusion.10
  95.0 2.3 convolution_add_fusion.9
  97.3 3.5 multiply_reduce_fusion.1
  100.9 14.2 %all-reduce.9 = (f32[128]{0:T(128)S(1)}, f32[]{:T(128)}, f32[128]{0:T(128)S(1)}) all-reduce(f32[128]{0:T(128)S(1)} %get-tuple-element.39, f32[]{:T(128)S(6)} %convert_element_type.118, f32[128]{0:T(128)S(1)} %get-tuple-element.38), channel_id=1, replica_groups=mesh['dp'=8,'chan'=4] {'dp'}, use_global_device_ids=true, to_apply=%region_1.2 | all-reduce | flops 257 | bytes 2056 | tf_op jit(solution)/shard_map/psum | solution.py:111
  116.8 2.4 fusion.371
  122.5 108.6 %all-gather.5.cloned.1.call-done = bf16[2,512,3072]{1,2,0:T(8,128)(2,1)} async-done(((bf16[2,128,3072]{1,2,0:T(8,128)(2,1)}), bf16[2,512,3072]{1,2,0:T(8,128)(2,1)}) %all-gather.5.cloned.1.call-update) | async-done | bytes 6291472 | tf_op jit(solution)/shard_map/all_gather | solution.py:125
  231.2 5.7 fusion.32
  238.8 2.1 convolution_add_fusion.6
  240.9 2.0 convolution_add_fusion.5
  244.8 2.0 convolution_add_fusion.3
  246.8 2.0 convolution_add_fusion.2
  248.9 3.4 convolution_add_fusion.1
  252.3 3.5 multiply_reduce_fusion
  255.8 14.0 %all-reduce.8 = (f32[128]{0:T(128)S(1)}, f32[128]{0:T(128)S(1)}) all-reduce(f32[128]{0:T(128)S(1)} %get-tuple-element.37, f32[128]{0:T(128)S(1)} %get-tuple-element.36), channel_id=1, replica_groups=mesh['dp'=8,'chan'=4] {'dp'}, use_global_device_ids=true, to_apply=%region_7.8 | all-reduce | flops 256 | bytes 2048 | tf_op jit(solution)/shard_map/psum | solution.py:128
  269.8 2.0 broadcast_in_dim.335
  271.8 4.9 fusion.404
  276.6 11.8 %all-reduce.7 = (f32[128]{0:T(128)S(1)}, f32[128]{0:T(128)S(1)}) all-reduce(f32[128]{0:T(128)S(1)} %get-tuple-element.44, f32[128]{0:T(128)S(1)} %get-tuple-element.43), channel_id=1, replica_groups=mesh['dp'=8,'chan'=4] {'dp'}, use_global_device_ids=true, to_apply=%region_13.14 | all-reduce | flops 256 | bytes 2048 | tf_op jit(solution)/shard_map/psum | solution.py:149
  288.5 3.5 fusion.12
  291.9 5.9 fusion.77
  297.8 5.8 fusion.74
  303.6 5.9 fusion.71
  309.6 5.8 fusion.66
  315.4 6.0 fusion.63
  321.4 5.8 fusion.60
  327.2 5.8 fusion.69
  333.0 5.9 fusion.80
  339.0 36.5 %add_bitcast_fusion = f32[2,512,3072]{1,2,0:T(8,128)} fusion(f32[2,3072,512]{2,1,0:T(8,128)} %fusion.60, f32[2,3072,512]{2,1,0:T(8,128)} %fusion.63, f32[2,3072,512]{2,1,0:T(8,128)} %fusion.66, f32[2,3072,512]{2,1,0:T(8,128)} %fusion.69, f32[2,3072,512]{2,1,0:T(8,128)} %fusion.71, f32[2,3072,512]{2,1,0:T(8,128)} %fusion.74, f32[2,3072,512]{2,1,0:T(8,128)} %fusion.80, ...), kind=kOutput, calls=%fused_computation | convolution fusion | flops 831258624 | bytes 114953216 | tf_op jit(solution)/shard_map/oi,nop->nip/dot_general | solution.py:37
  376.1 5.9 fusion.147
  382.1 5.4 fusion.161
  387.5 6.4 fusion.159
  393.9 2.3 fusion.157
  397.5 2.3 fusion.155
  399.9 2.3 fusion.153
  403.6 2.3 fusion.149
  405.9 177.9 %reduce-scatter.2.cloned.1.call-done = f32[2,128,3072]{1,2,0:T(8,128)} async-done(((f32[2,512,3072]{1,2,0:T(8,128)}), f32[2,128,3072]{1,2,0:T(8,128)}) %reduce-scatter.2.cloned.1.call-update) | async-done | bytes 3145744 | tf_op jit(solution)/shard_map/reduce_scatter | solution.py:162
  583.8 7.0 multiply_reduce_fusion.5
  590.8 14.4 %all-reduce.6 = (f32[128]{0:T(128)S(1)}, f32[128]{0:T(128)S(1)}, f32[]{:T(128)}) all-reduce(f32[128]{0:T(128)S(1)} %get-tuple-element.41, f32[128]{0:T(128)S(1)} %get-tuple-element.42, f32[]{:T(128)S(6)} %convert_element_type.130), channel_id=1, replica_groups=mesh['dp'=8,'chan'=4] {'dp'}, use_global_device_ids=true, to_apply=%region_18.19 | all-reduce | flops 257 | bytes 2056 | tf_op jit(solution)/shard_map/psum | solution.py:166
  605.2 3.4 fusion.11
  608.7 3.5 fusion.52
  612.2 3.7 fusion.49
  615.9 3.6 fusion.46
  619.5 3.5 fusion.41
  623.0 3.6 fusion.38
  626.6 3.6 fusion.55
  630.2 3.6 fusion.35
  633.8 3.7 fusion.44
  651.8 2.1 fusion.174
  654.9 19.0 %fusion = bf16[2,256,3072]{1,2,0:T(8,128)(2,1)} fusion(f32[2,3072,256]{2,1,0:T(8,128)} %fusion.35, f32[2,3072,256]{2,1,0:T(8,128)} %fusion.38, f32[2,3072,256]{2,1,0:T(8,128)} %fusion.41, f32[2,3072,256]{2,1,0:T(8,128)} %fusion.44, f32[2,3072,256]{2,1,0:T(8,128)} %fusion.46, f32[2,3072,256]{2,1,0:T(8,128)} %fusion.49, f32[2,3072,256]{2,1,0:T(8,128)} %fusion.55, ...), kind=kOutput, calls=%fused_computation.11 | convolution fusion | flops 417595392 | bytes 55118848 | tf_op jit(solution)/shard_map/oi,nop->nip/dot_general | solution.py:37
  673.9 8.8 %copy.106 = bf16[2,256,3072]{2,0,1:T(2,128)(2,1)} copy(bf16[2,256,3072]{1,2,0:T(8,128)(2,1)} %fusion) | data formatting | bytes 6291456 | tf_op jit(solution)/shard_map/convert_element_type | solution.py:172
  685.8 5.1 slice.236
  690.9 5.1 slice.237
  696.0 2.1 add_bitcast_fusion.1
  700.4 43.1 %all-reduce.5 = (f32[1]{0:T(128)}, f32[1]{0:T(128)}, f32[1]{0:T(128)}, f32[1]{0:T(128)}) all-reduce(f32[1]{0:T(128)} %bitcast.83, f32[1]{0:T(128)} %bitcast.82, f32[1]{0:T(128)} %bitcast.81, f32[1]{0:T(128)} %bitcast.80), channel_id=1, replica_groups=mesh['dp'=8,'chan'=4] {'dp','chan'}, use_global_device_ids=true, to_apply=%region_29.30 | all-reduce | flops 4 | bytes 32 | tf_op jit(solution)/shard_map/psum | solution.py:134
  744.2 3.1 fusion.315
  747.4 2.2 convert_element_type.127
  749.6 3.0 convert_element_type.128
  752.6 84.9 %all-reduce.14.cloned.1.call-done = bf16[2,256,3072]{2,0,1:T(2,128)(2,1)} async-done(((bf16[2,256,3072]{2,0,1:T(2,128)(2,1)}), bf16[2,256,3072]{2,0,1:T(2,128)(2,1)}) %all-reduce.14.cloned.1.call-update) | async-done | bytes 3145744
  (117 shorter events, 36.3 us)
Async XLA Ops:
  7.2 70.1 %all-gather.3.cloned.1.call-start = ((), (), s32[]{:S(2)}) async-start(), calls=%async_computation.1 | async-start | bytes 3932160 | tf_op jit(solution)/shard_map/all_gather | solution.py:108
  11.0 220.2 %all-gather.5.cloned.1.call-start = ((), (), s32[]{:S(2)}) async-start(), calls=%async_computation.2 | async-start | bytes 7864320 | tf_op jit(solution)/shard_map/all_gather | solution.py:125
  13.0 69.2 %copy-start.5 = (bf16[9,128,256]{2,1,0:T(8,128)(2,1)S(1)}, bf16[9,128,256]{2,1,0:T(8,128)(2,1)}, u32[]{:S(2)}) copy-start(bf16[9,128,256]{2,1,0:T(8,128)(2,1)} %param.11) | copy-start | bytes 1769476
  77.3 4.9 copy-start
  97.3 18.4 %copy-start.19 = (f32[128]{0:T(128)S(1)}, f32[128]{0:T(128)}, u32[]{:S(2)}) copy-start(f32[128]{0:T(128)} %param.12) | copy-start | bytes 1540
  97.3 19.5 %copy-start.21 = (f32[128]{0:T(128)S(1)}, f32[128]{0:T(128)}, u32[]{:S(2)}) copy-start(f32[128]{0:T(128)} %param.13) | copy-start | bytes 1540
  100.9 18.4 %copy-start.2 = (f32[2,3072,128]{2,1,0:T(8,128)}, f32[2,3072,128]{2,1,0:T(8,128)S(1)}, u32[]{:S(2)}) copy-start(f32[2,3072,128]{2,1,0:T(8,128)S(1)} %get-tuple-element.81) | copy-start | bytes 9437188
  116.2 0.5 copy-start.15
  116.2 0.6 copy-start.17
  116.8 2.5 copy-start.23
  119.2 464.5 %reduce-scatter.2.cloned.1.call-start = ((), (), s32[]{:S(2)}) async-start(), calls=%async_computation.3 | async-start | bytes 15728640 | tf_op jit(solution)/shard_map/reduce_scatter | solution.py:162
  119.4 0.6 copy-start.13
  120.1 1.2 copy-start.11
  122.5 114.4 %copy-start.8 = (bf16[9,128,512]{2,1,0:T(8,128)(2,1)S(1)}, bf16[9,128,512]{2,1,0:T(8,128)(2,1)}, u32[]{:S(2)}) copy-start(bf16[9,128,512]{2,1,0:T(8,128)(2,1)} %param.14) | copy-start | bytes 3538948
  231.2 5.7 copy-start.29
  252.3 17.5 %copy-start.24 = (f32[128]{0:T(128)S(1)}, f32[128]{0:T(128)}, u32[]{:S(2)}) copy-start(f32[128]{0:T(128)} %param.15) | copy-start | bytes 1540
  255.8 20.8 %copy-start.4 = (f32[2,3072,128]{2,1,0:T(8,128)}, f32[2,3072,128]{2,1,0:T(8,128)S(1)}, u32[]{:S(2)}) copy-start(f32[2,3072,128]{2,1,0:T(8,128)S(1)} %get-tuple-element.82) | copy-start | bytes 9437188
  255.8 15.9 %copy-start.26 = (f32[128]{0:T(128)S(1)}, f32[128]{0:T(128)}, u32[]{:S(2)}) copy-start(f32[128]{0:T(128)} %param.16) | copy-start | bytes 1540
  288.4 3.5 copy-start.27
  288.4 3.5 copy-start.31
  288.4 3.5 copy-start.9
  375.5 371.9 %all-reduce.16.cloned.1.call-start = ((), (), s32[]{:S(2)}) async-start(), calls=%async_computation.5 | async-start | bytes 3538944 | tf_op jit(solution)/shard_map/psum | solution.py:178
  382.1 11.8 %slice-start = ((s8[6291456]{0:T(1024)(128)(4,1)}), s8[4194304]{0:T(1024)(128)(4,1)S(1)}, s32[]{:S(2)}) async-start(s8[6291456]{0:T(1024)(128)(4,1)} %bitcast.413), calls=%async_computation.6 | async-start | bytes 8388608
  387.5 6.4 slice-start.1
  403.5 180.3 %copy-start.16 = (f32[128]{0:T(128)S(1)}, f32[128]{0:T(128)}, u32[]{:S(2)}) copy-start(f32[128]{0:T(128)} %copy-done.15) | copy-start | bytes 1540
  403.5 180.3 %copy-start.18 = (f32[128]{0:T(128)S(1)}, f32[128]{0:T(128)}, u32[]{:S(2)}) copy-start(f32[128]{0:T(128)} %copy-done.17) | copy-start | bytes 1540
  403.5 180.3 %copy-start.20 = (f32[128]{0:T(128)S(1)}, f32[128]{0:T(128)}, u32[]{:S(2)}) copy-start(f32[128]{0:T(128)} %param.12) | copy-start | bytes 1540
  403.5 180.2 %copy-start.22 = (f32[128]{0:T(128)S(1)}, f32[128]{0:T(128)}, u32[]{:S(2)}) copy-start(f32[128]{0:T(128)} %param.13) | copy-start | bytes 1540
  405.9 184.9 %copy-start.7 = (bf16[9,128,512]{2,1,0:T(8,128)(2,1)}, bf16[9,128,512]{2,1,0:T(8,128)(2,1)S(1)}, u32[]{:S(2)}) copy-start(bf16[9,128,512]{2,1,0:T(8,128)(2,1)S(1)} %fusion.149) | copy-start | bytes 3538948
  405.9 199.3 %copy-start.25 = (f32[128]{0:T(128)S(1)}, f32[128]{0:T(128)}, u32[]{:S(2)}) copy-start(f32[128]{0:T(128)} %get-tuple-element.69) | copy-start | bytes 1540
  605.2 3.5 copy-start.28
  605.2 3.5 copy-start.32
  605.2 3.5 copy-start.6
  633.8 3.7 copy-start.1
  653.9 0.9 copy-start.10
  654.8 182.6 %all-reduce.14.cloned.1.call-start = ((), (), s32[]{:S(2)}) async-start(), calls=%async_computation.4 | async-start | bytes 6291456
  682.6 0.7 copy-start.30
  682.6 3.2 copy-start.3
  690.9 7.2 copy-start.14
  696.0 3.2 copy-start.12
Sparse Core Ops, SparseCore 0:
  11.1 66.1 all-gather.2
  119.3 111.7 all-gather.4
  375.6 208.1 reduce-scatter.1
  654.9 59.5 all-reduce.15
  716.9 120.5 all-reduce.13
where the time goes:
time: 858 us; the launch traced here: 848 us
  waiting for transfers between devices  436 us (51%)
  matrix products  225 us (26%)
  blocking collectives  97.4 us (11%)
  other arithmetic  41.4 us (5%)
  local copies, waits for them, and re-layouts  28.2 us (3%)
  between operations  19.5 us (2%)
    reduce_scatter x1, waiting for transfers between devices, body(): lax.psum_scatter(convolve_back(second_grad, weight_mid), 'chan', scatter_...  178 us
    dot_general x18, matrix products, convolve_back(): jnp.einsum('oi,nop->nip', weight[tap], shifted(grads, 8 - tap), preferred...  131 us
    all_gather x1, waiting for transfers between devices, body(): lax.all_gather(first_act.astype(jnp.bfloat16), 'chan', axis=1, tiled=True)  109 us
    unnamed x6, waiting for transfers between devices  85 us
    all_gather x1, waiting for transfers between devices, body(): gathered_in = lax.all_gather(masked, 'chan', axis=1, tiled=True)  64.3 us
    dot_general x18, matrix products, convolve(): jnp.einsum('oi,nip->nop', weight[tap], shifted(field, tap), preferred_ele...  48.1 us
    dot_general x18, matrix products, weight_terms(): jnp.einsum('nop,nip->oi', grads, shifted(field, tap), preferred_element_t...  45.9 us
    psum x1, blocking collectives, body(): lax.psum((jnp.sum(masked_wide * masked_wide), jnp.sum(first_act * first_a...  43.1 us
  transfers between devices with their start and end apart: 5, of which 4 were waited for; matrix products, arithmetic and copies ran while one was open for 10% of the time, Pallas kernels for 0%

commit v1 on v0

v1 whole, which is shorter than its diff:
```python
import functools

import jax
import jax.numpy as jnp
from jax import lax
from jax.experimental import pallas as pl
from jax.experimental.pallas import tpu as pltpu
from jax.sharding import PartitionSpec as P

MEL = 8
HALO = 16
BF = jnp.bfloat16
F32 = jnp.float32
MIB = 1024 * 1024


class Geometry:
    def __init__(self, ndp, nch, clips, frames, c_in, c_mid):
        self.ndp, self.nch, self.ndev = ndp, nch, ndp * nch
        self.clips, self.frames = clips, frames
        self.ci_all, self.cm = c_in, c_mid
        self.ci, self.co = c_in // nch, c_mid // nch
        self.segs = nch // clips
        self.seg = frames // self.segs
        sides = min(self.segs - 1, 2)
        self.win = self.seg + HALO * sides
        self.starts = [
            min(max(s * self.seg - HALO, 0), frames - self.win) for s in range(self.segs)
        ]
        self.cwin = min(frames, (self.win + 48 + 63) // 64 * 64)
        self.cstarts = [min(s // 64 * 64, frames - self.cwin) for s in self.starts]
        self.rows = max(16, self.co // ndp)
        self.pieces = self.co // self.rows
        self.planes = self.pieces // 2


def dot(a, b, contract):
    return lax.dot_general(a, b, ((contract[0], contract[1]), ((), ())), preferred_element_type=F32)


def params(limit=56):
    return pltpu.CompilerParams(vmem_limit_bytes=limit * MIB)


def cost(flops, nbytes):
    return pl.CostEstimate(flops=int(flops), bytes_accessed=int(nbytes), transcendentals=0)


VMEM = pl.BlockSpec(memory_space=pltpu.VMEM)
SMEM = pl.BlockSpec(memory_space=pltpu.SMEM)
ANY = pl.BlockSpec(memory_space=pl.ANY)

LENGTH, START, OFF, QOFF, ZED, DEE = range(6)


def row_masks(g, info):
    r = lax.broadcasted_iota(jnp.int32, (g.win, 1), 0)
    valid = (r + info[START]) < info[LENGTH]
    own = valid & (r >= info[OFF]) & (r < info[OFF] + g.seg)
    return valid.astype(F32), own.astype(F32)


def shifted(x):
    n = x.shape[0]
    r = lax.broadcasted_iota(jnp.int32, (n, 1), 0)
    before = jnp.where(r == 0, 0.0, pltpu.roll(x, 1, 0))
    after = jnp.where(r == n - 1, 0.0, pltpu.roll(x, n - 1, 0))
    return before, after


def grid_order(rows=16):
    n = MEL * rows
    r = lax.broadcasted_iota(jnp.int32, (n, n), 0)
    c = lax.broadcasted_iota(jnp.int32, (n, n), 1)
    return (c == (r % rows) * MEL + r // rows).astype(BF)


def lanes(vector):
    n = vector.shape[1] // 128
    return jnp.concatenate([vector[:, 128 * i : 128 * (i + 1)] for i in range(n)], axis=0)


def unlanes(rows):
    return jnp.concatenate([rows[i : i + 1] for i in range(rows.shape[0])], axis=1)


def misc_row(*scalars):
    lane = lax.broadcasted_iota(jnp.int32, (1, 128), 1)
    row = jnp.zeros((1, 128), F32)
    for i, s in enumerate(scalars):
        row = jnp.where(lane == i, s, row)
    return row


def pick(row, i):
    lane = lax.broadcasted_iota(jnp.int32, (1, 128), 1)
    return jnp.sum(jnp.where(lane == i, row, 0.0), axis=1, keepdims=True)


def send_payload(ref, first, second, *extra):
    rows = [lanes(first), lanes(second), *extra]
    have = sum(r.shape[0] for r in rows)
    total = ref.shape[1]
    if have < total:
        rows.append(jnp.zeros((total - have, 128), F32))
    block = jnp.concatenate(rows, axis=0)
    ref[...] = jnp.broadcast_to(block[None], ref.shape)


def total_of(g, ref):
    n = g.cm // 128
    block = jnp.sum(ref[:, : 2 * n, :], axis=0)
    return unlanes(block[:n]), unlanes(block[n:])


def misc_of(g, ref):
    n = 2 * (g.cm // 128)
    return jnp.sum(ref[:, n, :], axis=0, keepdims=True)


def cut_kernel(g, info, spec, cot, w_in, w_mid, *rest):
    n = g.nch
    xs, cs, wi, wm, sems = rest[:n], rest[n : 2 * n], rest[2 * n], rest[2 * n + 1], rest[2 * n + 2]
    copies = []

    def add(src, dst):
        c = pltpu.make_async_copy(src, dst, sems.at[len(copies)])
        c.start()
        copies.append(c)

    piece = lax.rem(info[DEE], g.pieces)
    rows = pl.ds(pl.multiple_of(piece * g.rows, 16), g.rows)
    add(w_in.at[:, rows, :], wi)
    add(w_mid.at[:, rows, :], wm)
    for k in range(n):
        to = lax.rem(info[ZED] + k, n)
        clip, seg = to // g.segs, lax.rem(to, g.segs)
        start = jnp.clip(seg * g.seg - HALO, 0, g.frames - g.win)
        cstart = jnp.minimum(start // 64 * 64, g.frames - g.cwin)
        add(spec.at[clip, :, pl.ds(pl.multiple_of(start * MEL, 128), g.win * MEL)], xs[k])
        add(cot.at[clip, :, pl.ds(pl.multiple_of(cstart * 2, 128), g.cwin * 2)], cs[k])
    for c in copies:
        c.wait()


def cut(g, info, spec, cot, w_in, w_mid):
    n = g.nch
    shapes = (
        [jax.ShapeDtypeStruct((g.ci, g.win * MEL), BF)] * n
        + [jax.ShapeDtypeStruct((g.co, g.cwin * 2), BF)] * n
        + [
            jax.ShapeDtypeStruct((9, g.rows, g.ci_all), BF),
            jax.ShapeDtypeStruct((9, g.rows, g.cm), BF),
        ]
    )
    out = pl.pallas_call(
        functools.partial(cut_kernel, g),
        out_shape=shapes,
        in_specs=[SMEM] + [ANY] * 4,
        out_specs=[ANY] * len(shapes),
        scratch_shapes=[pltpu.SemaphoreType.DMA((2 * n + 2,))],
        compiler_params=params(8),
        name="cut",
    )(info, spec, cot, w_in, w_mid)
    return out[:n], out[n : 2 * n], out[2 * n], out[2 * n + 1]


def join_kernel(g, info, own, *rest):
    parts, out = rest[:-1], rest[-1]
    z = info[ZED]
    out[:, pl.ds(pl.multiple_of(z * g.co, 16), g.co), :] = own[...]
    for q in range(g.pieces):
        piece = lax.rem(info[DEE], g.pieces) ^ q
        for k in range(1, g.nch):
            source = lax.rem(z + g.nch - k, g.nch)
            at = pl.multiple_of(source * g.co + piece * g.rows, 16)
            out[:, pl.ds(at, g.rows), :] = parts[q][k - 1]


def join(g, info, own, parts, depth, name):
    return pl.pallas_call(
        functools.partial(join_kernel, g),
        out_shape=jax.ShapeDtypeStruct((9, g.cm, depth), BF),
        in_specs=[SMEM] + [VMEM] * (1 + len(parts)),
        out_specs=VMEM,
        compiler_params=params(24),
        cost_estimate=cost(0, 4 * 9 * g.cm * depth),
        name=name,
    )(info, own, *parts)


def conv_rows(m, x3, weight):
    total = None
    for b in range(3):
        if 0 <= m + b - 1 < MEL:
            term = dot(x3[m + b - 1], weight(b), ((1,), (1,)))
            total = term if total is None else total + term
    return total


def conv_back_rows(m, g3, weight):
    total = None
    for b in range(3):
        if 0 <= m - b + 1 < MEL:
            term = dot(g3[m - b + 1], weight(b), ((1,), (0,)))
            total = term if total is None else total + term
    return total


def side_by_side(ref):
    return lambda b: jnp.concatenate([ref[b], ref[3 + b], ref[6 + b]], axis=1)


def stacked(ref):
    return lambda b: jnp.concatenate([ref[b], ref[3 + b], ref[6 + b]], axis=0)


def first_kernel(g, info, lens, gains, *rest):
    n = g.nch
    xs, w, pre, x3, pay, held = rest[:n], rest[n], rest[n + 1], rest[n + 2], rest[n + 3], rest[n + 4]
    c = g.ci_all
    for k in range(n):
        source = lax.rem(info[ZED] + n - k, n)
        held[pl.ds(pl.multiple_of(source * g.ci, 16), g.ci), :] = xs[k][...]
    valid, own = row_masks(g, info)
    order = grid_order()
    square = jnp.zeros((1, c), F32)
    for j in range(g.win // 16):
        block = dot(order, held[:, 128 * j : 128 * (j + 1)], ((1,), (1,)))
        v = valid[16 * j : 16 * (j + 1)]
        o = own[16 * j : 16 * (j + 1)]
        for m in range(MEL):
            part = block[16 * m : 16 * (m + 1)] * v
            square = square + jnp.sum(part * part * o, axis=0, keepdims=True)
            x3[m, 16 * j : 16 * (j + 1), c : 2 * c] = part.astype(BF)
    for m in range(MEL):
        before, after = shifted(x3[m, :, c : 2 * c].astype(F32))
        x3[m, :, 0:c] = before.astype(BF)
        x3[m, :, 2 * c : 3 * c] = after.astype(BF)
    one = jnp.zeros((1, g.cm), F32)
    two = jnp.zeros((1, g.cm), F32)
    weight = side_by_side(w)
    for m in range(MEL):
        total = conv_rows(m, x3, weight)
        pre[m] = total
        kept = total * own
        one = one + jnp.sum(kept, axis=0, keepdims=True)
        two = two + jnp.sum(kept * total, axis=0, keepdims=True)
    frame_total = 0
    pair_total = 0
    for i in range(g.clips):
        frame_total = frame_total + lens[i]
        pair_total = pair_total + (lens[i] + 1) // 2
    row = misc_row(
        frame_total.astype(F32), pair_total.astype(F32), jnp.sum(square, axis=1, keepdims=True)
    )
    send_payload(pay, one, two, row, gains[...])


def first(g, info, lens, gains, xs, w):
    return pl.pallas_call(
        functools.partial(first_kernel, g),
        out_shape=[
            jax.ShapeDtypeStruct((MEL, g.win, g.cm), F32),
            jax.ShapeDtypeStruct((MEL, g.win, 3 * g.ci_all), BF),
            jax.ShapeDtypeStruct((g.ndev, 16, 128), F32),
        ],
        in_specs=[SMEM, SMEM] + [VMEM] * (2 + g.nch),
        out_specs=[VMEM] * 3,
        scratch_shapes=[pltpu.VMEM((g.ci_all, g.win * MEL), BF)],
        compiler_params=params(32),
        cost_estimate=cost(2 * 9 * MEL * g.win * g.ci_all * g.cm, 10 * MIB),
        name="first_conv",
    )(info, lens, gains, *xs, w)


MEAN1, INV1, GAMMA1, BETA1, GAMMA2, BETA2, COUNT, PAIRS, SQ0, MEAN2, INV2, SQ1 = range(12)
TABLE = 16


def second_kernel(g, info, got, pre1, w, pre, x3, table, pay):
    c = g.cm
    one, two = total_of(g, got)
    misc = misc_of(g, got)
    count = MEL * pick(misc, 0) / g.nch
    pairs = (MEL // 2) * pick(misc, 1) / g.nch
    at = 2 * (c // 128) + 1
    vectors = [
        jnp.concatenate([got[zz, at + i : at + i + 1, : g.co] for zz in range(g.nch)], axis=1)
        for i in range(4)
    ]
    gamma, beta = vectors[0], vectors[1]
    mean = one / count
    inverse = lax.rsqrt(two / count - mean * mean + 1e-05)
    wide = jnp.zeros((1, c), F32)
    table[...] = jnp.concatenate(
        [mean, inverse, *vectors, wide + count, wide + pairs, wide + pick(misc, 2)]
        + [wide] * (TABLE - 9),
        axis=0,
    )
    valid, own = row_masks(g, info)
    square = jnp.zeros((1, c), F32)
    for m in range(MEL):
        affine = gamma * ((pre1[m] - mean) * inverse) + beta
        act = affine / (1.0 + jnp.exp(-affine)) * valid
        square = square + jnp.sum(act * act * own, axis=0, keepdims=True)
        low = act.astype(BF)
        before, after = shifted(low.astype(F32))
        x3[m, :, 0:c] = before.astype(BF)
        x3[m, :, c : 2 * c] = low
        x3[m, :, 2 * c : 3 * c] = after.astype(BF)
    one = jnp.zeros((1, c), F32)
    two = jnp.zeros((1, c), F32)
    weight = side_by_side(w)
    for m in range(MEL):
        total = conv_rows(m, x3, weight)
        pre[m] = total
        kept = total * own
        one = one + jnp.sum(kept, axis=0, keepdims=True)
        two = two + jnp.sum(kept * total, axis=0, keepdims=True)
    send_payload(pay, one, two, misc_row(jnp.sum(square, axis=1, keepdims=True)))


def second(g, info, got, pre1, w):
    return pl.pallas_call(
        functools.partial(second_kernel, g),
        out_shape=[
            jax.ShapeDtypeStruct((MEL, g.win, g.cm), F32),
            jax.ShapeDtypeStruct((MEL, g.win, 3 * g.cm), BF),
            jax.ShapeDtypeStruct((TABLE, g.cm), F32),
            jax.ShapeDtypeStruct((g.ndev, 16, 128), F32),
        ],
        in_specs=[SMEM] + [VMEM] * 3,
        out_specs=[VMEM] * 4,
        compiler_params=params(40),
        cost_estimate=cost(2 * 9 * MEL * g.win * g.cm * g.cm, 17 * MIB),
        name="second_conv",
    )(info, got, pre1, w)


def pool_kernel(g, info, got, table1, pre2, *rest):
    n, c = g.nch, g.cm
    cs, outs = rest[:n], rest[n : 2 * n]
    local_ref, table, pay, held, grads, pooled_ref, flat = rest[2 * n :]
    one, two = total_of(g, got)
    misc = misc_of(g, got)
    old = table1[...]
    count = old[COUNT : COUNT + 1]
    gamma, beta = old[GAMMA2 : GAMMA2 + 1], old[BETA2 : BETA2 + 1]
    mean = one / count
    inverse = lax.rsqrt(two / count - mean * mean + 1e-05)
    wide = jnp.zeros((1, c), F32)
    table[...] = jnp.concatenate(
        [old[:MEAN2], mean, inverse, wide + pick(misc, 0)] + [wide] * (TABLE - 12), axis=0
    )
    for k in range(n):
        source = lax.rem(info[ZED] + n - k, n)
        held[pl.ds(pl.multiple_of(source * g.co, 16), g.co), :] = cs[k][...]
    r = lax.broadcasted_iota(jnp.int32, (256, 128), 0)
    l = lax.broadcasted_iota(jnp.int32, (256, 128), 1)
    spread = (l == (r % 64) // 2 * 4 + r // 64).astype(BF)
    for j in range(g.cwin // 64):
        block = dot(spread, held[:, 128 * j : 128 * (j + 1)], ((1,), (1,)))
        for k in range(MEL // 2):
            grads[k, 64 * j : 64 * (j + 1), :] = block[64 * k : 64 * (k + 1)]
    valid, own = row_masks(g, info)
    r = lax.broadcasted_iota(jnp.int32, (g.win, 1), 0) + info[START]
    share = jnp.where(info[LENGTH] - r // 2 * 2 >= 2, 0.25, 0.5)
    window = pl.ds(pl.multiple_of(info[QOFF], 16), g.win)
    segment = pl.ds(pl.multiple_of(info[OFF], 16), g.seg)
    beta_sum = gamma_sum = square = jnp.zeros((1, c), F32)
    for k in range(MEL // 2):
        given = grads[k, window, :] * (share * valid)
        pair = None
        for m in (2 * k, 2 * k + 1):
            scaled = (pre2[m] - mean) * inverse
            affine = gamma * scaled + beta
            sigma = 1.0 / (1.0 + jnp.exp(-affine))
            act = affine * sigma * valid
            square = square + jnp.sum(act * act * own, axis=0, keepdims=True)
            local = given * sigma * (1.0 + affine * (1.0 - sigma))
            local_ref[m] = local
            kept = local * own
            beta_sum = beta_sum + jnp.sum(kept, axis=0, keepdims=True)
            gamma_sum = gamma_sum + jnp.sum(kept * scaled, axis=0, keepdims=True)
            pair = act if pair is None else pair + act
        pooled_ref[k] = pair * share
    wide_rows = (MEL // 2) * g.seg
    values = jnp.concatenate([pooled_ref[k, segment, :] for k in range(MEL // 2)], axis=0)
    high = values.astype(BF)
    low = (values - high.astype(F32)).astype(BF)
    r = lax.broadcasted_iota(jnp.int32, (wide_rows, 2 * g.seg), 0)
    l = lax.broadcasted_iota(jnp.int32, (wide_rows, 2 * g.seg), 1)
    gather = (l == (r % g.seg) // 2 * 4 + r // g.seg).astype(BF)
    pooled = dot(high, gather, ((0,), (0,))) + dot(low, gather, ((0,), (0,)))
    flat[...] = pooled.astype(BF)
    pooled_square = jnp.sum(jnp.sum(pooled * pooled, axis=1, keepdims=True), axis=0, keepdims=True)
    for k in range(n):
        to = lax.rem(info[ZED] + k, n)
        outs[k][...] = flat[pl.ds(pl.multiple_of(to * g.co, 16), g.co), :]
    send_payload(
        pay, beta_sum, gamma_sum, misc_row(jnp.sum(square, axis=1, keepdims=True), pooled_square)
    )


def pool(g, info, got, table1, pre2, cs):
    n = g.nch
    out = pl.pallas_call(
        functools.partial(pool_kernel, g),
        out_shape=[jax.ShapeDtypeStruct((g.co, 2 * g.seg), BF)] * n
        + [
            jax.ShapeDtypeStruct((MEL, g.win, g.cm), F32),
            jax.ShapeDtypeStruct((TABLE, g.cm), F32),
            jax.ShapeDtypeStruct((g.ndev, 16, 128), F32),
        ],
        in_specs=[SMEM] + [VMEM] * (3 + n),
        out_specs=[VMEM] * (n + 3),
        scratch_shapes=[
            pltpu.VMEM((g.cm, g.cwin * 2), BF),
            pltpu.VMEM((MEL // 2, g.cwin, g.cm), F32),
            pltpu.VMEM((MEL // 2, g.win, g.cm), F32),
            pltpu.VMEM((g.cm, 2 * g.seg), BF),
        ],
        compiler_params=params(40),
        cost_estimate=cost(4e9, 8 * MIB),
        name="pool",
    )(info, got, table1, pre2, *cs)
    return out[:n], out[n], out[n + 1], out[n + 2]


def back_kernel(g, info, got, table, pre2, local2, pre1, w, local1, grad, roots, sums, pay, g3):
    c = g.cm
    beta_sum, gamma_sum = total_of(g, got)
    misc = misc_of(g, got)
    t = table[...]

    def row(i):
        return t[i : i + 1]

    count = row(COUNT)
    sums[...] = jnp.concatenate([beta_sum, gamma_sum] + [jnp.zeros((1, c), F32)] * 6, axis=0)
    one = count[:, :128]
    pairs = t[PAIRS : PAIRS + 1, :128]
    lane = lax.broadcasted_iota(jnp.int32, (1, 128), 1)
    tops = misc_row(pick(t[SQ0 : SQ0 + 1, :128], 0), pick(t[SQ1 : SQ1 + 1, :128], 0))
    tops = jnp.where(lane == 2, pick(misc, 0), jnp.where(lane == 3, pick(misc, 1), tops))
    under = jnp.where(lane == 0, one * g.ci_all, jnp.where(lane == 3, pairs * c, one * c))
    roots[...] = jnp.broadcast_to(jnp.sqrt(tops / under), (8, 128))
    valid, own = row_masks(g, info)
    factor = row(GAMMA2) * row(INV2)
    beta_part, gamma_part = beta_sum / count, gamma_sum / count
    for m in range(MEL):
        scaled = (pre2[m] - row(MEAN2)) * row(INV2)
        value = valid * (factor * (local2[m] - beta_part - scaled * gamma_part))
        low = value.astype(BF)
        before, after = shifted(low.astype(F32))
        g3[m, :, 0:c] = after.astype(BF)
        g3[m, :, c : 2 * c] = low
        g3[m, :, 2 * c : 3 * c] = before.astype(BF)
        grad[m] = (value * own).astype(BF)
    weight = stacked(w)
    beta_sum = gamma_sum = jnp.zeros((1, c), F32)
    for m in range(MEL):
        given = conv_back_rows(m, g3, weight)
        scaled = (pre1[m] - row(MEAN1)) * row(INV1)
        affine = row(GAMMA1) * scaled + row(BETA1)
        sigma = 1.0 / (1.0 + jnp.exp(-affine))
        local = given * valid * sigma * (1.0 + affine * (1.0 - sigma))
        local1[m] = local
        kept = local * own
        beta_sum = beta_sum + jnp.sum(kept, axis=0, keepdims=True)
        gamma_sum = gamma_sum + jnp.sum(kept * scaled, axis=0, keepdims=True)
    send_payload(pay, beta_sum, gamma_sum)


def back(g, info, got, table, pre2, local2, pre1, w):
    return pl.pallas_call(
        functools.partial(back_kernel, g),
        out_shape=[
            jax.ShapeDtypeStruct((MEL, g.win, g.cm), F32),
            jax.ShapeDtypeStruct((MEL, g.win, g.cm), BF),
            jax.ShapeDtypeStruct((8, 128), F32),
            jax.ShapeDtypeStruct((8, g.cm), F32),
            jax.ShapeDtypeStruct((g.ndev, 8, 128), F32),
        ],
        in_specs=[SMEM] + [VMEM] * 6,
        out_specs=[VMEM] * 5,
        scratch_shapes=[pltpu.VMEM((MEL, g.win, 3 * g.cm), BF)],
        compiler_params=params(44),
        cost_estimate=cost(2 * 9 * MEL * g.win * g.cm * g.cm, 20 * MIB),
        name="second_back",
    )(info, got, table, pre2, local2, pre1, w)


def weight_terms(g, info, grad, x3, depth, keep, give):
    core = lax.rem(info[DEE], 2)
    for tap in range(9):
        a, b = tap // 3, tap % 3
        low = max(0, 1 - b)
        high = min(MEL, MEL + 1 - b)
        rows = (high - low) * g.win
        left = grad[low:high].reshape(rows, g.cm)
        right = x3[low + b - 1 : high + b - 1, :, a * depth : (a + 1) * depth].reshape(rows, depth)
        term = dot(left, right, ((0,), (0,))).astype(BF)

        for mine in range(2):

            @pl.when(core == mine)
            def _():
                for z in range(g.nch):
                    for p in range(g.pieces):
                        at = z * g.co + p * g.rows
                        to = keep if p % 2 == mine else give
                        to[p // 2, z, tap] = term[at : at + g.rows]


def pieces_shape(g, depth):
    return jax.ShapeDtypeStruct((g.planes, g.nch, 9, g.rows, depth), BF)


def mid_terms_kernel(g, info, grad, x3, keep, give):
    weight_terms(g, info, grad, x3, g.cm, keep, give)


def mid_terms(g, info, grad, x3):
    return pl.pallas_call(
        functools.partial(mid_terms_kernel, g),
        out_shape=[pieces_shape(g, g.cm)] * 2,
        in_specs=[SMEM, VMEM, VMEM],
        out_specs=[VMEM] * 2,
        compiler_params=params(40),
        cost_estimate=cost(2 * 9 * MEL * g.win * g.cm * g.cm, 12 * MIB),
        name="weight_mid_terms",
    )(info, grad, x3)


def in_terms_kernel(g, info, got, table, pre1, local1, x3, grad, keep, give, sums, own_grad):
    beta_sum, gamma_sum = total_of(g, got)
    t = table[...]
    mean, inverse, gamma = t[MEAN1 : MEAN1 + 1], t[INV1 : INV1 + 1], t[GAMMA1 : GAMMA1 + 1]
    count = t[COUNT : COUNT + 1]
    sums[...] = jnp.concatenate([beta_sum, gamma_sum] + [jnp.zeros((1, g.cm), F32)] * 6, axis=0)
    valid, own = row_masks(g, info)
    factor = gamma * inverse
    beta_part, gamma_part = beta_sum / count, gamma_sum / count
    for m in range(MEL):
        scaled = (pre1[m] - mean) * inverse
        value = valid * (factor * (local1[m] - beta_part - scaled * gamma_part))
        grad[m] = value.astype(BF)
        own_grad[m] = (value * own).astype(BF)
    weight_terms(g, info, own_grad, x3, g.ci_all, keep, give)


def in_terms(g, info, got, table, pre1, local1, x3):
    return pl.pallas_call(
        functools.partial(in_terms_kernel, g),
        out_shape=[
            jax.ShapeDtypeStruct((MEL, g.win, g.cm), BF),
            pieces_shape(g, g.ci_all),
            pieces_shape(g, g.ci_all),
            jax.ShapeDtypeStruct((8, g.cm), F32),
        ],
        in_specs=[SMEM] + [VMEM] * 5,
        out_specs=[VMEM] * 4,
        scratch_shapes=[pltpu.VMEM((MEL, g.win, g.cm), BF)],
        compiler_params=params(40),
        cost_estimate=cost(2 * 9 * MEL * g.win * g.cm * g.ci_all, 14 * MIB),
        name="weight_in_terms",
    )(info, got, table, pre1, local1, x3)


def spectra_kernel(g, info, grad, w, *rest):
    n, c = g.nch, g.cm
    outs, g3, rows, flat = rest[:n], rest[n], rest[n + 1], rest[n + 2]
    for m in range(MEL):
        low = grad[m]
        before, after = shifted(low.astype(F32))
        g3[m, :, 0:c] = after.astype(BF)
        g3[m, :, c : 2 * c] = low
        g3[m, :, 2 * c : 3 * c] = before.astype(BF)
    valid, own = row_masks(g, info)
    weight = stacked(w)
    for m in range(MEL):
        rows[m] = (conv_back_rows(m, g3, weight) * own).astype(BF)
    order = grid_order()
    for j in range(g.seg // 16):
        at = pl.ds(pl.multiple_of(info[OFF] + 16 * j, 16), 16)
        block = jnp.concatenate([rows[m, at, :] for m in range(MEL)], axis=0)
        flat[:, 128 * j : 128 * (j + 1)] = dot(block, order, ((0,), (0,))).astype(BF)
    for k in range(n):
        to = lax.rem(info[ZED] + k, n)
        outs[k][...] = flat[pl.ds(pl.multiple_of(to * g.ci, 16), g.ci), :]


def spectra_back(g, info, grad, w):
    n = g.nch
    return pl.pallas_call(
        functools.partial(spectra_kernel, g),
        out_shape=[jax.ShapeDtypeStruct((g.ci, g.seg * MEL), BF)] * n,
        in_specs=[SMEM, VMEM, VMEM],
        out_specs=[VMEM] * n,
        scratch_shapes=[
            pltpu.VMEM((MEL, g.win, 3 * g.cm), BF),
            pltpu.VMEM((MEL, g.win, g.ci_all), BF),
            pltpu.VMEM((g.ci_all, g.seg * MEL), BF),
        ],
        compiler_params=params(40),
        cost_estimate=cost(2 * 9 * MEL * g.win * g.cm * g.ci_all, 5 * MIB),
        name="spectra_back",
    )(info, grad, w)


def place_kernel(g, width, info, *rest):
    n = g.nch
    parts, out = rest[:n], rest[n]
    for k in range(n):
        source = lax.rem(info[ZED] + n - k, n)
        for zz in range(n):

            @pl.when(source == zz)
            def _():
                seg = zz % g.segs
                out[zz // g.segs, :, seg * width : (seg + 1) * width] = parts[k][...].astype(
                    out.dtype
                )


def place(g, info, parts, dtype, name):
    channels, width = parts[0].shape
    return pl.pallas_call(
        functools.partial(place_kernel, g, width),
        out_shape=jax.ShapeDtypeStruct((g.clips, channels, g.segs * width), dtype),
        in_specs=[SMEM] + [VMEM] * g.nch,
        out_specs=VMEM,
        compiler_params=params(16),
        name=name,
    )(info, *parts)


def core_sum_kernel(g, info, keep, got, *outs):
    plane = lax.rem(info[DEE], g.pieces) // 2
    for j in range(g.planes):
        at = plane ^ j
        outs[j][...] = (keep[at].astype(F32) + got[at].astype(F32)).astype(BF)


def core_sum(g, info, keep, got, name):
    shape = keep.shape[1:]
    return pl.pallas_call(
        functools.partial(core_sum_kernel, g),
        out_shape=[jax.ShapeDtypeStruct(shape, BF)] * g.planes,
        in_specs=[SMEM, VMEM, VMEM],
        out_specs=[VMEM] * g.planes,
        compiler_params=params(16),
        name=name,
    )(info, keep, got)


def plane_sum_kernel(g, info, *rest):
    parts, outs = rest[: g.planes], rest[g.planes :]
    for k in range(g.nch):
        to = lax.rem(info[ZED] + k, g.nch)
        total = parts[0][to].astype(F32)
        for p in parts[1:]:
            total = total + p[to].astype(F32)
        outs[k][...] = total.astype(BF)


def plane_sum(g, info, parts, name):
    shape = parts[0].shape[1:]
    return pl.pallas_call(
        functools.partial(plane_sum_kernel, g),
        out_shape=[jax.ShapeDtypeStruct(shape, BF)] * g.nch,
        in_specs=[SMEM] + [VMEM] * g.planes,
        out_specs=[VMEM] * g.nch,
        compiler_params=params(16),
        name=name,
    )(info, *parts)


def chan_sum_kernel(*refs):
    total = refs[0][...].astype(F32)
    for r in refs[1:-1]:
        total = total + r[...].astype(F32)
    refs[-1][...] = total.astype(BF)


def chan_sum(g, parts, name):
    return pl.pallas_call(
        chan_sum_kernel,
        out_shape=jax.ShapeDtypeStruct(parts[0].shape, BF),
        in_specs=[VMEM] * len(parts),
        out_specs=VMEM,
        compiler_params=params(16),
        name=name,
    )(*parts)


def spread_kernel(g, info, *rest):
    parts, out = rest[:-1], rest[-1]
    for q in range(g.pieces):
        piece = lax.rem(info[DEE], g.pieces) ^ q
        at = pl.multiple_of(piece * g.rows, 16)
        out[:, pl.ds(at, g.rows), :] = parts[q][...].astype(F32)


def spread_out(g, info, parts, depth, name):
    return pl.pallas_call(
        functools.partial(spread_kernel, g),
        out_shape=jax.ShapeDtypeStruct((9, g.co, depth), F32),
        in_specs=[SMEM] + [VMEM] * g.pieces,
        out_specs=VMEM,
        compiler_params=params(16),
        name=name,
    )(info, *parts)


class Links:
    def __init__(self, g):
        self.g = g

    def swap(self, x, bits):
        return lax.ppermute(x, "dp", [(i, i ^ bits) for i in range(self.g.ndp)])

    def along(self, x, k):
        n = self.g.nch
        return lax.ppermute(x, "chan", [(i, (i + k) % n) for i in range(n)])

    def exchange(self, parts):
        return [parts[0]] + [self.along(parts[k], k) for k in range(1, self.g.nch)]

    def gather_pieces(self, x):
        have = [x] + [None] * (self.g.pieces - 1)
        for q in range(2, self.g.pieces, 2):
            have[q] = self.swap(x, q)
        for q in range(1, self.g.pieces, 2):
            have[q] = self.swap(have[q - 1], 1)
        return have

    def whole_weight(self, info, own, piece, depth, name):
        parts = jnp.stack([self.along(piece, k) for k in range(1, self.g.nch)])
        return join(self.g, info, own, self.gather_pieces(parts), depth, name)

    def weight_sum(self, info, keep, give, depth, name):
        g = self.g
        parts = core_sum(g, info, keep, self.swap(give, 1), name + "_core_sum")
        parts = [parts[0]] + [self.swap(parts[j], 2 * j) for j in range(1, g.planes)]
        bit = g.pieces
        parts = plane_sum(g, info, parts, name + "_plane_sum")
        parts = self.exchange(parts)
        mine = chan_sum(g, parts, name + "_chan_sum")
        while bit < g.ndp:
            mine = chan_sum(g, [mine, self.swap(mine, bit)], name + "_rest_sum")
            bit *= 2
        return spread_out(g, info, self.gather_pieces(mine), depth, name + "_out")


def everyone(x):
    return lax.all_to_all(x, ("dp", "chan"), 0, 0)


def make_body(ndp, nch):
    def body(
        spectra, lengths, weight_in, gamma_in, beta_in, weight_mid, gamma_mid, beta_mid, cotangent
    ):
        g = Geometry(
            ndp,
            nch,
            spectra.shape[0],
            spectra.shape[2] // MEL,
            weight_in.shape[2],
            weight_mid.shape[2],
        )
        links = Links(g)
        z = lax.axis_index("chan")
        d = lax.axis_index("dp")
        seg = z % g.segs
        start = jnp.clip(seg * g.seg - HALO, 0, g.frames - g.win)
        cstart = jnp.minimum(start // 64 * 64, g.frames - g.cwin)
        length = lax.dynamic_index_in_dim(lengths, z // g.segs, keepdims=False)
        info = jnp.stack(
            [length, start, seg * g.seg - start, start - cstart, z, d, z * 0, z * 0]
        ).astype(jnp.int32)
        gains = jnp.stack([gamma_in, beta_in, gamma_mid, beta_mid])
        gains = jnp.pad(gains, ((0, 0), (0, 128 - g.co)))

        xs, cs, piece_in, piece_mid = cut(g, info, spectra, cotangent, weight_in, weight_mid)
        w_in = links.whole_weight(info, weight_in, piece_in, g.ci_all, "join_in")
        xs = links.exchange(xs)
        w_mid = links.whole_weight(info, weight_mid, piece_mid, g.cm, "join_mid")
        cs = links.exchange(cs)

        pre1, x3_in, pay = first(g, info, lengths, gains, xs, w_in)
        got = everyone(pay)
        pre2, x3_mid, table, pay = second(g, info, got, pre1, w_mid)
        got = everyone(pay)
        pooled, local2, table, pay = pool(g, info, got, table, pre2, cs)
        pooled = links.exchange(pooled)
        got = everyone(pay)
        local1, grad2, roots, sums2, pay = back(g, info, got, table, pre2, local2, pre1, w_mid)
        got = everyone(pay)
        keep_mid, give_mid = mid_terms(g, info, grad2, x3_mid)
        grad1, keep_in, give_in, sums1 = in_terms(g, info, got, table, pre1, local1, x3_in)
        parts = spectra_back(g, info, grad1, w_in)
        weight_mid_grad = links.weight_sum(info, keep_mid, give_mid, g.cm, "mid")
        weight_in_grad = links.weight_sum(info, keep_in, give_in, g.ci_all, "in")
        parts = links.exchange(parts)
        spectra_grad = place(g, info, parts, F32, "place_spectra")
        block_out = place(g, info, pooled, BF, "place_pooled")

        def share(sums, i):
            return lax.dynamic_slice_in_dim(sums[i], z * g.co, g.co)

        return (
            block_out,
            spectra_grad,
            weight_in_grad,
            share(sums1, 1),
            share(sums1, 0),
            weight_mid_grad,
            share(sums2, 1),
            share(sums2, 0),
            roots[0, :4],
        )

    return body


def solution(mesh):
    placed = (
        P("dp", "chan", None),
        P("dp"),
        P(None, "chan", None),
        P("chan"),
        P("chan"),
        P(None, "chan", None),
        P("chan"),
        P("chan"),
        P("dp", "chan", None),
    )
    return jax.shard_map(
        make_body(mesh.shape["dp"], mesh.shape["chan"]),
        mesh=mesh,
        in_specs=placed,
        out_specs=(
            P("dp", "chan", None),
            P("dp", "chan", None),
            P(None, "chan", None),
            P("chan"),
            P("chan"),
            P(None, "chan", None),
            P("chan"),
            P("chan"),
            P(),
        ),
        check_vma=False,
    )
```

time: 858 us -> 327 us (0.38)
  waiting for transfers between devices: 436 us -> 93.2 us
  matrix products: 225 us -> 0 us
  Pallas kernels: 0 us -> 83.3 us
  blocking collectives: 97.4 us -> 27.1 us
  starting transfers between devices: 0.21 us -> 68.9 us
  other arithmetic: 41.4 us -> 0.85 us
  between operations: 19.5 us -> 1.35 us
  local copies, waits for them, and re-layouts: 28.2 us -> 46.1 us
    dot_general x54 -> x0, matrix products: 225 us -> none  [the longest x18 131 us: convolve_back(): jnp.einsum('oi,nop->nip', weight[tap], shifted(grads, 8 - tap), preferred...]
    reduce_scatter x1 -> x0, waiting for transfers between devices: 178 us -> none  [body(): lax.psum_scatter(convolve_back(second_grad, weight_mid), 'chan', scatter_...]
    all_gather x2 -> x0, waiting for transfers between devices: 173 us -> none  [the longest x1 109 us: body(): lax.all_gather(first_act.astype(jnp.bfloat16), 'chan', axis=1, tiled=True)]
    psum x5 -> x0, blocking collectives: 97.4 us -> none  [the longest x1 43.1 us: body(): lax.psum((jnp.sum(masked_wide * masked_wide), jnp.sum(first_act * first_a...]
    ppermute x0 -> x60, waiting for transfers between devices: none -> 91 us  [the longest x24 63.3 us: along(): return lax.ppermute(x, 'chan', [(i, (i + k) % n) for i in range(n)])]
    unnamed x6 -> x0, waiting for transfers between devices: 85 us -> none
    pallas_call x0 -> x20, Pallas kernels: none -> 83.3 us  [the longest x1 14.6 us: second(): pl.pallas_call(functools.partial(second_kernel, g), out_shape=[jax.ShapeD...]
    ppermute x0 -> x60, starting transfers between devices: none -> 57.6 us  [the longest x24 32.1 us: along(): return lax.ppermute(x, 'chan', [(i, (i + k) % n) for i in range(n)])]
  transfers between devices with their start and end apart: 5 -> 62, of which waited for: 4 -> 21; matrix products, arithmetic and copies ran while one was open for 10% -> 1% of each run, Pallas kernels for 0% -> 11%
where the time goes in v1:
time: 327 us; the launch traced here: 321 us
  waiting for transfers between devices  93.2 us (29%)
  Pallas kernels  83.3 us (25%)
  starting transfers between devices  68.9 us (21%)
  local copies, waits for them, and re-layouts  46.1 us (14%)
  blocking collectives  27.1 us (8%)
    ppermute x24, waiting for transfers between devices, along(): return lax.ppermute(x, 'chan', [(i, (i + k) % n) for i in range(n)])  63.3 us
    unnamed x104, local copies, waits for them, and re-layouts  41 us
    ppermute x24, starting transfers between devices, along(): return lax.ppermute(x, 'chan', [(i, (i + k) % n) for i in range(n)])  32.1 us
    ppermute x36, waiting for transfers between devices, swap(): return lax.ppermute(x, 'dp', [(i, i ^ bits) for i in range(self.g.ndp)])  27.6 us
    all_to_all x2, blocking collectives, everyone(): return lax.all_to_all(x, ('dp', 'chan'), 0, 0)  27.1 us
    ppermute x36, starting transfers between devices, swap(): return lax.ppermute(x, 'dp', [(i, i ^ bits) for i in range(self.g.ndp)])  25.5 us
    pallas_call x1, Pallas kernels, second(): pl.pallas_call(functools.partial(second_kernel, g), out_shape=[jax.ShapeD...  14.6 us
    pallas_call x1, Pallas kernels, back(): pl.pallas_call(functools.partial(back_kernel, g), out_shape=[jax.ShapeDty...  12.8 us
  transfers between devices with their start and end apart: 62, of which 21 were waited for; matrix products, arithmetic and copies ran while one was open for 1% of the time, Pallas kernels for 11%

profile of v1, /device:TPU:0, one launch (start us, length us, event | category | flops | bytes accessed | tf_op | source)
XLA Modules:
  0.0 320.9 jit_solution(17729831425209756103)
XLA Ops:
  8.8 5.0 %collective-permute-start.5 = (bf16[9,16,256]{2,1,0:T(8,128)(2,1)S(1)}, bf16[9,16,256]{2,1,0:T(8,128)(2,1)S(1)}, u32[]{:S(2)}, u32[]{:S(2)}) collective-permute-start(bf16[9,16,256]{2,1,0:T(8,128)(2,1)S(1)} %get-tuple-element.68), channel_id=1, source_target_pairs={{0,3},{1,0},{2,1},{3,2},{4,7},{5,4},{6,5},{7,6},{8,11},{9,8},{10,9... | collective-permute-start | bytes 221192 | tf_op jit(solution)/shard_map/ppermute | solution.py:727
  14.9 2.8 collective-permute-start.15
  18.8 2.3 collective-permute-done.4
  21.1 2.5 collective-permute-start.11
  24.8 8.7 %collective-permute-done.14 = bf16[9,16,512]{2,1,0:T(8,128)(2,1)S(1)} collective-permute-done((bf16[9,16,512]{2,1,0:T(8,128)(2,1)S(1)}, bf16[9,16,512]{2,1,0:T(8,128)(2,1)S(1)}, u32[]{:S(2)}, u32[]{:S(2)}) %collective-permute-start.14) | collective-permute-done | bytes 147488 | tf_op jit(solution)/shard_map/ppermute | solution.py:727
  34.6 8.4 %collective-permute-done.rest_1_ = bf16[64,1664]{1,0:T(8,128)(2,1)S(1)} collective-permute-done((bf16[64,1664]{1,0:T(8,128)(2,1)S(1)}, bf16[64,1664]{1,0:T(8,128)(2,1)S(1)}, u32[]{:S(2)}, u32[]{:S(2)}) %collective-permute-start) | collective-permute-done | bytes 213024 | tf_op jit(solution)/shard_map/ppermute | solution.py:727
  44.7 2.4 collective-permute-start.21
  48.9 4.7 %collective-permute-done.1.rest_2_ = bf16[64,1664]{1,0:T(8,128)(2,1)S(1)} collective-permute-done((bf16[64,1664]{1,0:T(8,128)(2,1)S(1)}, bf16[64,1664]{1,0:T(8,128)(2,1)S(1)}, u32[]{:S(2)}, u32[]{:S(2)}) %collective-permute-start.1) | collective-permute-done | bytes 213024 | tf_op jit(solution)/shard_map/ppermute | solution.py:727
  54.5 6.7 %first_conv.1 = (f32[8,208,512]{2,1,0:T(8,128)S(1)}, bf16[8,208,768]{2,1,0:T(8,128)(2,1)S(1)}, f32[32,16,128]{2,1,0:T(8,128)S(1)}) custom-call(s32[8]{0:T(128)S(1)} %stack.63.info, s32[2]{0:T(128)S(1)} %copy-done.31, f32[4,128]{1,0:T(4,128)S(1)} %pad_maximum_fusion.2.gains, bf16[64,1664]{1,0:T(8,128)(2,1)S(1)} %get-tuple-element.64.rest_0_, ...), custom_call_target="tpu_custom_call" | custom-call | flops 3925868544 | bytes 10485760 | tf_op jit(solution)/shard_map/first_conv/pallas_call | solution.py:261
  61.9 1.8 copy-done.32
  63.7 1.5 copy-done.37
  65.1 7.6 %all-to-all-start = ((f32[32,16,128]{2,1,0:T(8,128)}), f32[32,16,128]{2,1,0:T(8,128)}, u32[]{:S(2)}, u32[]{:S(2)}) async-start(f32[32,16,128]{2,1,0:T(8,128)} %copy-done.12), calls=%async_computation | async-start | bytes 524288 | tf_op jit(solution)/shard_map/all_to_all | solution.py:759
  76.8 1.7 join_mid.1.w
  78.5 2.2 copy-done.2
  80.7 2.2 all-to-all-done.got
  82.9 2.3 copy-done.3
  85.3 2.0 copy-done.33
  87.3 14.6 %second_conv.1 = (f32[8,208,512]{2,1,0:T(8,128)S(1)}, bf16[8,208,1536]{2,1,0:T(8,128)(2,1)}, f32[16,512]{1,0:T(8,128)S(1)}, f32[32,16,128]{2,1,0:T(8,128)}) custom-call(s32[8]{0:T(128)S(1)} %stack.63.info, f32[32,16,128]{2,1,0:T(8,128)} %all-to-all-done.got, f32[8,208,512]{2,1,0:T(8,128)S(1)} %copy-done.33, bf16[9,512,512]{2,1,0:T(8,128)(2,1)S(1)} %copy-done.3), custom_call_target="tpu_custom_call" | custom-call | flops 7851737088 | bytes 17825792 | tf_op jit(solution)/shard_map/second_conv/pallas_call | solution.py:325
  101.9 1.7 copy-done.41
  104.2 3.7 %all-to-all-start.1 = ((f32[32,16,128]{2,1,0:T(8,128)}), f32[32,16,128]{2,1,0:T(8,128)S(1)}, u32[]{:S(2)}, u32[]{:S(2)}) async-start(f32[32,16,128]{2,1,0:T(8,128)} %get-tuple-element.72), calls=%async_computation.1 | async-start | bytes 524288 | tf_op jit(solution)/shard_map/all_to_all | solution.py:759
  107.9 1.8 collective-permute-start.23
  109.7 2.4 collective-permute-start.24
  112.2 1.7 collective-permute-start.25
  113.8 6.3 %collective-permute-done.23.rest_1_ = bf16[128,512]{1,0:T(8,128)(2,1)S(1)} collective-permute-done((bf16[128,512]{1,0:T(8,128)(2,1)S(1)}, bf16[128,512]{1,0:T(8,128)(2,1)S(1)}, u32[]{:S(2)}, u32[]{:S(2)}) %collective-permute-start.23) | collective-permute-done | bytes 131104 | tf_op jit(solution)/shard_map/ppermute | solution.py:727
  120.1 6.1 %collective-permute-done.24.rest_2_ = bf16[128,512]{1,0:T(8,128)(2,1)S(1)} collective-permute-done((bf16[128,512]{1,0:T(8,128)(2,1)S(1)}, bf16[128,512]{1,0:T(8,128)(2,1)S(1)}, u32[]{:S(2)}, u32[]{:S(2)}) %collective-permute-start.24) | collective-permute-done | bytes 131104 | tf_op jit(solution)/shard_map/ppermute | solution.py:727
  126.2 2.0 copy-done.42
  128.9 6.3 %pool.1 = (bf16[128,384]{1,0:T(8,128)(2,1)S(1)}, bf16[128,384]{1,0:T(8,128)(2,1)S(1)}, bf16[128,384]{1,0:T(8,128)(2,1)S(1)}, bf16[128,384]{1,0:T(8,128)(2,1)S(1)...) custom-call(s32[8]{0:T(128)S(1)} %stack.63.info, ...), custom_call_target="tpu_custom_call" | custom-call | flops 4000000000 | bytes 8388608 | tf_op jit(solution)/shard_map/pool/pallas_call | solution.py:408
  135.3 1.7 copy-done.44
  137.0 16.5 %all_to_all.20.got = f32[32,16,128]{2,1,0:T(8,128)S(1)} all-to-all(f32[32,16,128]{2,1,0:T(8,128)S(1)} %get-tuple-element.83), channel_id=1, replica_groups=mesh['dp'=8,'chan'=4] {'dp','chan'}, dimensions={0} | all-to-all | bytes 524288 | tf_op jit(solution)/shard_map/all_to_all | solution.py:759
  153.5 12.8 %second_back.1 = (f32[8,208,512]{2,1,0:T(8,128)S(1)}, bf16[8,208,512]{2,1,0:T(8,128)(2,1)S(1)}, f32[8,128]{1,0:T(8,128)S(1)}, f32[8,512]{1,0:T(8,128)S(1)}, f32[32,8,128]{2,1,0:T(8,128)S(1)}) custom-call(s32[8]{0:T(128)S(1)} %stack.63.info, f32[32,16,128]{2,1,0:T(8,128)S(1)} %all_to_all.20.got, f32[16,512]{1,0:T(8,128)S(1)} %get-tuple-element.84.table, ...), custom_call_target="tpu_custom_call" | custom-call | flops 7851737088 | bytes 20971520 | tf_op jit(solution)/shard_map/second_back/pallas_call | solution.py:477
  166.3 1.8 copy-done.35
  168.1 2.5 copy-done.45
  170.5 10.5 %weight_mid_terms.1 = (bf16[4,4,9,16,512]{4,3,2,1,0:T(8,128)(2,1)S(1)}, bf16[4,4,9,16,512]{4,3,2,1,0:T(8,128)(2,1)S(1)}) custom-call(s32[8]{0:T(128)S(1)} %stack.63.info, bf16[8,208,512]{2,1,0:T(8,128)(2,1)S(1)} %get-tuple-element.105.grad, bf16[8,208,1536]{2,1,0:T(8,128)(2,1)S(1)} %copy-done.45), custom_call_target="tpu_custom_call" | custom-call | flops 7851737088 | bytes 12582912 | tf_op jit(solution)/shard_map/weight_mid_terms/pallas_call | solution.py:526
  181.6 10.6 %all_to_all.21.got = f32[32,8,128]{2,1,0:T(8,128)S(1)} all-to-all(f32[32,8,128]{2,1,0:T(8,128)S(1)} %get-tuple-element.86), channel_id=1, replica_groups=mesh['dp'=8,'chan'=4] {'dp','chan'}, dimensions={0} | all-to-all | bytes 262144 | tf_op jit(solution)/shard_map/all_to_all | solution.py:759
  192.2 2.0 copy-done.34
  194.2 2.0 copy-done.36
  196.2 1.7 copy-done.38
  197.9 10.4 %weight_in_terms.1 = (bf16[8,208,512]{2,1,0:T(8,128)(2,1)S(1)}, bf16[4,4,9,16,256]{4,3,2,1,0:T(8,128)(2,1)S(1)}, bf16[4,4,9,16,256]{4,3,2,1,0:T(8,128)(2,1)S(1)}, f32[8,512]{1,0:T(8,128)S(1)}) custom-call(s32[8]{0:T(128)S(1)} %stack.63.info, f32[32,8,128]{2,1,0:T(8,128)S(1)} %all_to_all.21.got, f32[16,512]{1,0:T(8,128)S(1)} %get-tuple-element.84.table, ...), custom_call_target="tpu_custom_call" | custom-call | flops 3925868544 | bytes 14680064 | tf_op jit(solution)/shard_map/weight_in_terms/pallas_call | solution.py:555
  209.2 2.5 collective-permute-done.32.got
  211.7 1.6 in_core_sum.1
  214.0 2.1 mid_core_sum.1
  218.2 1.4 collective-permute-start.49
  220.6 6.1 %collective-permute-done.27.rest_2_ = bf16[128,384]{1,0:T(8,128)(2,1)S(1)} collective-permute-done((bf16[128,384]{1,0:T(8,128)(2,1)S(1)}, bf16[128,384]{1,0:T(8,128)(2,1)S(1)}, u32[]{:S(2)}, u32[]{:S(2)}) %collective-permute-start.27) | collective-permute-done | bytes 98336 | tf_op jit(solution)/shard_map/ppermute | solution.py:727
  227.3 1.5 collective-permute-start.28
  228.8 3.1 collective-permute-done.28.rest_3_
  233.8 2.1 collective-permute-start.35
  239.5 1.4 place_pooled.1
  240.9 18.3 %collective-permute-done.34.rest_2_ = bf16[4,9,16,256]{3,2,1,0:T(8,128)(2,1)} collective-permute-done((bf16[4,9,16,256]{3,2,1,0:T(8,128)(2,1)}, bf16[4,9,16,256]{3,2,1,0:T(8,128)(2,1)}, u32[]{:S(2)}, u32[]{:S(2)}) %collective-permute-start.34) | collective-permute-done | bytes 294944 | tf_op jit(solution)/shard_map/ppermute | solution.py:723
  262.6 2.8 collective-permute-start.37
  266.4 1.5 mid_plane_sum.1
  270.4 4.9 %spectra_back.1 = (bf16[64,1536]{1,0:T(8,128)(2,1)S(1)}, bf16[64,1536]{1,0:T(8,128)(2,1)S(1)}, bf16[64,1536]{1,0:T(8,128)(2,1)S(1)}, bf16[64,1536]{1,0:T(8,128)(2,1)S(1)}) custom-call(s32[8]{0:T(128)S(1)} %stack.63.info, bf16[8,208,512]{2,1,0:T(8,128)(2,1)S(1)} %copy-done.40, bf16[9,512,256]{2,1,0:T(8,128)(2,1)S(1)} %join_in.1.rest_4_.w), custom_call_target="tpu_custom_call" | custom-call | flops 3925868544 | bytes 5242880 | tf_op jit(solution)/shard_map/spectra_back/pallas_call | solution.py:597
  275.2 2.3 collective-permute-start.29
  280.1 1.5 collective-permute-start.44
  281.6 8.5 %collective-permute-done.51.refs_2_ = bf16[9,16,512]{2,1,0:T(8,128)(2,1)S(1)} collective-permute-done((bf16[9,16,512]{2,1,0:T(8,128)(2,1)S(1)}, bf16[9,16,512]{2,1,0:T(8,128)(2,1)S(1)}, u32[]{:S(2)}, u32[]{:S(2)}) %collective-permute-start.51) | collective-permute-done | bytes 147488 | tf_op jit(solution)/shard_map/ppermute | solution.py:727
  290.1 2.1 collective-permute-start.52
  293.0 8.5 %collective-permute-done.52.refs_3_ = bf16[9,16,512]{2,1,0:T(8,128)(2,1)S(1)} collective-permute-done((bf16[9,16,512]{2,1,0:T(8,128)(2,1)S(1)}, bf16[9,16,512]{2,1,0:T(8,128)(2,1)S(1)}, u32[]{:S(2)}, u32[]{:S(2)}) %collective-permute-start.52) | collective-permute-done | bytes 147488 | tf_op jit(solution)/shard_map/ppermute | solution.py:727
  301.6 2.1 collective-permute-start.40
  303.7 1.4 collective-permute-start.58
  305.3 1.9 collective-permute-start.54
  309.5 1.9 collective-permute-done.58.rest_6_
  311.4 1.7 collective-permute-done.56.rest_4_
  315.0 1.9 place_spectra.1
  316.9 1.6 in_out.1
  318.6 2.1 mid_out.1
  (197 shorter events, 48.6 us)
Async XLA Ops:
  0.6 47.5 %copy-start.48 = (f32[128]{0:T(128)S(1)}, f32[128]{0:T(128)}, u32[]{:S(2)}) copy-start(f32[128]{0:T(128)} %param.16) | copy-start | bytes 1540
  0.7 47.5 %copy-start.49 = (f32[128]{0:T(128)S(1)}, f32[128]{0:T(128)}, u32[]{:S(2)}) copy-start(f32[128]{0:T(128)} %param.15) | copy-start | bytes 1540
  8.8 10.0 %collective-permute-start.5 = (bf16[9,16,256]{2,1,0:T(8,128)(2,1)S(1)}, bf16[9,16,256]{2,1,0:T(8,128)(2,1)S(1)}, u32[]{:S(2)}, u32[]{:S(2)}) collective-permute-start(bf16[9,16,256]{2,1,0:T(8,128)(2,1)S(1)} %get-tuple-element.68), channel_id=1, source_target_pairs={{0,3},{1,0},{2,1},{3,2},{4,7},{5,4},{6,5},{7,6},{8,11},{9,8},{10,9... | collective-permute-start | bytes 221192 | tf_op jit(solution)/shard_map/ppermute | solution.py:727
  13.8 7.2 %collective-permute-start.4 = (bf16[9,16,256]{2,1,0:T(8,128)(2,1)S(1)}, bf16[9,16,256]{2,1,0:T(8,128)(2,1)S(1)}, u32[]{:S(2)}, u32[]{:S(2)}) collective-permute-start(bf16[9,16,256]{2,1,0:T(8,128)(2,1)S(1)} %get-tuple-element.68), channel_id=1, source_target_pairs={{0,2},{1,3},{2,0},{3,1},{4,6},{5,7},{6,4},{7,5},{8,10},{9,11},{10,... | collective-permute-start | bytes 221192 | tf_op jit(solution)/shard_map/ppermute | solution.py:727
  13.9 7.2 %collective-permute-start.3 = (bf16[9,16,256]{2,1,0:T(8,128)(2,1)S(1)}, bf16[9,16,256]{2,1,0:T(8,128)(2,1)S(1)}, u32[]{:S(2)}, u32[]{:S(2)}) collective-permute-start(bf16[9,16,256]{2,1,0:T(8,128)(2,1)S(1)} %get-tuple-element.68), channel_id=1, source_target_pairs={{0,1},{1,2},{2,3},{3,0},{4,5},{5,6},{6,7},{7,4},{8,9},{9,10},{10,1... | collective-permute-start | bytes 221192 | tf_op jit(solution)/shard_map/ppermute | solution.py:727
  14.9 9.3 %collective-permute-start.15 = (bf16[9,16,512]{2,1,0:T(8,128)(2,1)S(1)}, bf16[9,16,512]{2,1,0:T(8,128)(2,1)S(1)}, u32[]{:S(2)}, u32[]{:S(2)}) collective-permute-start(bf16[9,16,512]{2,1,0:T(8,128)(2,1)S(1)} %get-tuple-element.71), channel_id=1, source_target_pairs={{0,3},{1,0},{2,1},{3,2},{4,7},{5,4},{6,5},{7,6},{8,11},{9,8},{10,9... | collective-permute-start | bytes 442376 | tf_op jit(solution)/shard_map/ppermute | solution.py:727
  17.7 15.9 %collective-permute-start.14 = (bf16[9,16,512]{2,1,0:T(8,128)(2,1)S(1)}, bf16[9,16,512]{2,1,0:T(8,128)(2,1)S(1)}, u32[]{:S(2)}, u32[]{:S(2)}) collective-permute-start(bf16[9,16,512]{2,1,0:T(8,128)(2,1)S(1)} %get-tuple-element.71), channel_id=1, source_target_pairs={{0,2},{1,3},{2,0},{3,1},{4,6},{5,7},{6,4},{7,5},{8,10},{9,11},{10,... | collective-permute-start | bytes 442376 | tf_op jit(solution)/shard_map/ppermute | solution.py:727
  18.8 14.7 %collective-permute-start.13 = (bf16[9,16,512]{2,1,0:T(8,128)(2,1)S(1)}, bf16[9,16,512]{2,1,0:T(8,128)(2,1)S(1)}, u32[]{:S(2)}, u32[]{:S(2)}) collective-permute-start(bf16[9,16,512]{2,1,0:T(8,128)(2,1)S(1)} %get-tuple-element.71), channel_id=1, source_target_pairs={{0,1},{1,2},{2,3},{3,0},{4,5},{5,6},{6,7},{7,4},{8,9},{9,10},{10,1... | collective-permute-start | bytes 442376 | tf_op jit(solution)/shard_map/ppermute | solution.py:727
  21.1 12.5 %collective-permute-start.11 = (bf16[3,9,16,256]{3,2,1,0:T(8,128)(2,1)S(1)}, bf16[3,9,16,256]{3,2,1,0:T(8,128)(2,1)S(1)}, u32[]{:S(2)}, u32[]{:S(2)}) collective-permute-start(bf16[3,9,16,256]{3,2,1,0:T(8,128)(2,1)S(1)} %pad_maximum_fusion.1.rest_0_), channel_id=1, source_target_pairs={{0,24},{4,28},{8,16},{12,20},{16,8},{20,12},{24,0},{28,4},{1,25},{... | collective-permute-start | bytes 663560 | tf_op jit(solution)/shard_map/ppermute | solution.py:723
  23.6 10.5 %collective-permute-start.9 = (bf16[3,9,16,256]{3,2,1,0:T(8,128)(2,1)S(1)}, bf16[3,9,16,256]{3,2,1,0:T(8,128)(2,1)S(1)}, u32[]{:S(2)}, u32[]{:S(2)}) collective-permute-start(bf16[3,9,16,256]{3,2,1,0:T(8,128)(2,1)S(1)} %pad_maximum_fusion.1.rest_0_), channel_id=1, source_target_pairs={{0,16},{4,20},{8,24},{12,28},{16,0},{20,4},{24,8},{28,12},{1,17},{... | collective-permute-start | bytes 663560 | tf_op jit(solution)/shard_map/ppermute | solution.py:723
  24.1 10.1 %collective-permute-start.7 = (bf16[3,9,16,256]{3,2,1,0:T(8,128)(2,1)S(1)}, bf16[3,9,16,256]{3,2,1,0:T(8,128)(2,1)S(1)}, u32[]{:S(2)}, u32[]{:S(2)}) collective-permute-start(bf16[3,9,16,256]{3,2,1,0:T(8,128)(2,1)S(1)} %pad_maximum_fusion.1.rest_0_), channel_id=1, source_target_pairs={{0,8},{4,12},{8,0},{12,4},{16,24},{20,28},{24,16},{28,20},{1,9},{5... | collective-permute-start | bytes 663560 | tf_op jit(solution)/shard_map/ppermute | solution.py:723
  33.5 9.5 %collective-permute-start.6 = (bf16[3,9,16,256]{3,2,1,0:T(8,128)(2,1)S(1)}, bf16[3,9,16,256]{3,2,1,0:T(8,128)(2,1)S(1)}, u32[]{:S(2)}, u32[]{:S(2)}) collective-permute-start(bf16[3,9,16,256]{3,2,1,0:T(8,128)(2,1)S(1)} %pad_maximum_fusion.1.rest_0_), channel_id=1, source_target_pairs={{0,4},{4,0},{8,12},{12,8},{16,20},{20,16},{24,28},{28,24},{1,5},{5... | collective-permute-start | bytes 663560 | tf_op jit(solution)/shard_map/ppermute | solution.py:723
  33.5 9.5 %collective-permute-start = (bf16[64,1664]{1,0:T(8,128)(2,1)S(1)}, bf16[64,1664]{1,0:T(8,128)(2,1)S(1)}, u32[]{:S(2)}, u32[]{:S(2)}) collective-permute-start(bf16[64,1664]{1,0:T(8,128)(2,1)S(1)} %get-tuple-element.65), channel_id=1, source_target_pairs={{0,1},{1,2},{2,3},{3,0},{4,5},{5,6},{6,7},{7,4},{8,9},{9,10},{10,1... | collective-permute-start | bytes 638984 | tf_op jit(solution)/shard_map/ppermute | solution.py:727
  33.6 11.1 %collective-permute-start.12 = (bf16[3,9,16,256]{3,2,1,0:T(8,128)(2,1)S(1)}, bf16[3,9,16,256]{3,2,1,0:T(8,128)(2,1)S(1)}, u32[]{:S(2)}, u32[]{:S(2)}) collective-permute-start(bf16[3,9,16,256]{3,2,1,0:T(8,128)(2,1)S(1)} %collective-permute-done.11.rest_6_), channel_id=1, source_target_pairs={{0,4},{4,0},{8,12},{12,8},{16,20},{20,16},{24,28},{28,24},{1,5},{5... | collective-permute-start | bytes 663560 | tf_op jit(solution)/shard_map/ppermute | solution.py:723
  34.1 13.0 %collective-permute-start.10 = (bf16[3,9,16,256]{3,2,1,0:T(8,128)(2,1)S(1)}, bf16[3,9,16,256]{3,2,1,0:T(8,128)(2,1)S(1)}, u32[]{:S(2)}, u32[]{:S(2)}) collective-permute-start(bf16[3,9,16,256]{3,2,1,0:T(8,128)(2,1)S(1)} %collective-permute-done.9.rest_4_), channel_id=1, source_target_pairs={{0,4},{4,0},{8,12},{12,8},{16,20},{20,16},{24,28},{28,24},{1,5},{5... | collective-permute-start | bytes 663560 | tf_op jit(solution)/shard_map/ppermute | solution.py:723
  34.2 13.4 %collective-permute-start.8 = (bf16[3,9,16,256]{3,2,1,0:T(8,128)(2,1)S(1)}, bf16[3,9,16,256]{3,2,1,0:T(8,128)(2,1)S(1)}, u32[]{:S(2)}, u32[]{:S(2)}) collective-permute-start(bf16[3,9,16,256]{3,2,1,0:T(8,128)(2,1)S(1)} %collective-permute-done.7.rest_2_), channel_id=1, source_target_pairs={{0,4},{4,0},{8,12},{12,8},{16,20},{20,16},{24,28},{28,24},{1,5},{5... | collective-permute-start | bytes 663560 | tf_op jit(solution)/shard_map/ppermute | solution.py:723
  43.0 10.6 %collective-permute-start.1 = (bf16[64,1664]{1,0:T(8,128)(2,1)S(1)}, bf16[64,1664]{1,0:T(8,128)(2,1)S(1)}, u32[]{:S(2)}, u32[]{:S(2)}) collective-permute-start(bf16[64,1664]{1,0:T(8,128)(2,1)S(1)} %get-tuple-element.66), channel_id=1, source_target_pairs={{0,2},{1,3},{2,0},{3,1},{4,6},{5,7},{6,4},{7,5},{8,10},{9,11},{10,... | collective-permute-start | bytes 638984 | tf_op jit(solution)/shard_map/ppermute | solution.py:727
  43.0 11.4 %collective-permute-start.2 = (bf16[64,1664]{1,0:T(8,128)(2,1)S(1)}, bf16[64,1664]{1,0:T(8,128)(2,1)S(1)}, u32[]{:S(2)}, u32[]{:S(2)}) collective-permute-start(bf16[64,1664]{1,0:T(8,128)(2,1)S(1)} %get-tuple-element.67), channel_id=1, source_target_pairs={{0,3},{1,0},{2,1},{3,2},{4,7},{5,4},{6,5},{7,6},{8,11},{9,8},{10,9... | collective-permute-start | bytes 638984 | tf_op jit(solution)/shard_map/ppermute | solution.py:727
  44.7 28.5 %collective-permute-start.21 = (bf16[3,9,16,512]{3,2,1,0:T(8,128)(2,1)}, bf16[3,9,16,512]{3,2,1,0:T(8,128)(2,1)}, u32[]{:S(2)}, u32[]{:S(2)}) collective-permute-start(bf16[3,9,16,512]{3,2,1,0:T(8,128)(2,1)} %pad_maximum_fusion.rest_0_), channel_id=1, source_target_pairs={{0,24},{4,28},{8,16},{12,20},{16,8},{20,12},{24,0},{28,4},{1,25},{... | collective-permute-start | bytes 1327112 | tf_op jit(solution)/shard_map/ppermute | solution.py:723
  47.1 26.2 %collective-permute-start.19 = (bf16[3,9,16,512]{3,2,1,0:T(8,128)(2,1)}, bf16[3,9,16,512]{3,2,1,0:T(8,128)(2,1)}, u32[]{:S(2)}, u32[]{:S(2)}) collective-permute-start(bf16[3,9,16,512]{3,2,1,0:T(8,128)(2,1)} %pad_maximum_fusion.rest_0_), channel_id=1, source_target_pairs={{0,16},{4,20},{8,24},{12,28},{16,0},{20,4},{24,8},{28,12},{1,17},{... | collective-permute-start | bytes 1327112 | tf_op jit(solution)/shard_map/ppermute | solution.py:723
  47.6 26.1 %collective-permute-start.17 = (bf16[3,9,16,512]{3,2,1,0:T(8,128)(2,1)}, bf16[3,9,16,512]{3,2,1,0:T(8,128)(2,1)}, u32[]{:S(2)}, u32[]{:S(2)}) collective-permute-start(bf16[3,9,16,512]{3,2,1,0:T(8,128)(2,1)} %pad_maximum_fusion.rest_0_), channel_id=1, source_target_pairs={{0,8},{4,12},{8,0},{12,4},{16,24},{20,28},{24,16},{28,20},{1,9},{5... | collective-permute-start | bytes 1327112 | tf_op jit(solution)/shard_map/ppermute | solution.py:723
  65.1 17.8 %all-to-all-start = ((f32[32,16,128]{2,1,0:T(8,128)}), f32[32,16,128]{2,1,0:T(8,128)}, u32[]{:S(2)}, u32[]{:S(2)}) async-start(f32[32,16,128]{2,1,0:T(8,128)} %copy-done.12), calls=%async_computation | async-start | bytes 524288 | tf_op jit(solution)/shard_map/all_to_all | solution.py:759
  72.8 2.1 collective-permute-start.16
  73.2 2.3 collective-permute-start.22
  73.4 2.8 collective-permute-start.20
  73.7 3.0 collective-permute-start.18
  104.2 22.0 %all-to-all-start.1 = ((f32[32,16,128]{2,1,0:T(8,128)}), f32[32,16,128]{2,1,0:T(8,128)S(1)}, u32[]{:S(2)}, u32[]{:S(2)}) async-start(f32[32,16,128]{2,1,0:T(8,128)} %get-tuple-element.72), calls=%async_computation.1 | async-start | bytes 524288 | tf_op jit(solution)/shard_map/all_to_all | solution.py:759
  107.9 12.2 %collective-permute-start.23 = (bf16[128,512]{1,0:T(8,128)(2,1)S(1)}, bf16[128,512]{1,0:T(8,128)(2,1)S(1)}, u32[]{:S(2)}, u32[]{:S(2)}) collective-permute-start(bf16[128,512]{1,0:T(8,128)(2,1)S(1)} %copy-done.30), channel_id=1, source_target_pairs={{0,1},{1,2},{2,3},{3,0},{4,5},{5,6},{6,7},{7,4},{8,9},{9,10},{10,1... | collective-permute-start | bytes 393224 | tf_op jit(solution)/shard_map/ppermute | solution.py:727
  109.7 16.4 %collective-permute-start.24 = (bf16[128,512]{1,0:T(8,128)(2,1)S(1)}, bf16[128,512]{1,0:T(8,128)(2,1)S(1)}, u32[]{:S(2)}, u32[]{:S(2)}) collective-permute-start(bf16[128,512]{1,0:T(8,128)(2,1)S(1)} %copy-done.28), channel_id=1, source_target_pairs={{0,2},{1,3},{2,0},{3,1},{4,6},{5,7},{6,4},{7,5},{8,10},{9,11},{10,... | collective-permute-start | bytes 393224 | tf_op jit(solution)/shard_map/ppermute | solution.py:727
  112.2 14.0 %collective-permute-start.25 = (bf16[128,512]{1,0:T(8,128)(2,1)S(1)}, bf16[128,512]{1,0:T(8,128)(2,1)S(1)}, u32[]{:S(2)}, u32[]{:S(2)}) collective-permute-start(bf16[128,512]{1,0:T(8,128)(2,1)S(1)} %copy-done.26), channel_id=1, source_target_pairs={{0,3},{1,0},{2,1},{3,2},{4,7},{5,4},{6,5},{7,6},{8,11},{9,8},{10,9... | collective-permute-start | bytes 393224 | tf_op jit(solution)/shard_map/ppermute | solution.py:727
  181.1 32.9 %collective-permute-start.46 = (bf16[4,4,9,16,512]{4,3,2,1,0:T(8,128)(2,1)S(1)}, bf16[4,4,9,16,512]{4,3,2,1,0:T(8,128)(2,1)S(1)}, u32[]{:S(2)}, u32[]{:S(2)}) collective-permute-start(bf16[4,4,9,16,512]{4,3,2,1,0:T(8,128)(2,1)S(1)} %get-tuple-element.108), channel_id=1, source_target_pairs={{0,4},{4,0},{8,12},{12,8},{16,20},{20,16},{24,28},{28,24},{1,5},{5... | collective-permute-start | bytes 7077896 | tf_op jit(solution)/shard_map/ppermute | solution.py:723
  208.9 2.8 collective-permute-start.32
  208.9 10.8 %collective-permute-start.26 = (bf16[128,384]{1,0:T(8,128)(2,1)S(1)}, bf16[128,384]{1,0:T(8,128)(2,1)S(1)}, u32[]{:S(2)}, u32[]{:S(2)}) collective-permute-start(bf16[128,384]{1,0:T(8,128)(2,1)S(1)} %get-tuple-element.80), channel_id=1, source_target_pairs={{0,1},{1,2},{2,3},{3,0},{4,5},{5,6},{6,7},{7,4},{8,9},{9,10},{10,1... | collective-permute-start | bytes 294920 | tf_op jit(solution)/shard_map/ppermute | solution.py:727
  213.3 19.8 %collective-permute-start.33 = (bf16[4,9,16,256]{3,2,1,0:T(8,128)(2,1)S(1)}, bf16[4,9,16,256]{3,2,1,0:T(8,128)(2,1)S(1)}, u32[]{:S(2)}, u32[]{:S(2)}) collective-permute-start(bf16[4,9,16,256]{3,2,1,0:T(8,128)(2,1)S(1)} %get-tuple-element.97), channel_id=1, source_target_pairs={{0,8},{4,12},{8,0},{12,4},{16,24},{20,28},{24,16},{28,20},{1,9},{5... | collective-permute-start | bytes 884744 | tf_op jit(solution)/shard_map/ppermute | solution.py:723
  216.1 49.2 %collective-permute-start.47 = (bf16[4,9,16,512]{3,2,1,0:T(8,128)(2,1)}, bf16[4,9,16,512]{3,2,1,0:T(8,128)(2,1)S(1)}, u32[]{:S(2)}, u32[]{:S(2)}) collective-permute-start(bf16[4,9,16,512]{3,2,1,0:T(8,128)(2,1)} %get-tuple-element.110), channel_id=1, source_target_pairs={{0,8},{4,12},{8,0},{12,4},{16,24},{20,28},{24,16},{28,20},{1,9},{5... | collective-permute-start | bytes 1769480 | tf_op jit(solution)/shard_map/ppermute | solution.py:723
  217.4 49.0 %collective-permute-start.48 = (bf16[4,9,16,512]{3,2,1,0:T(8,128)(2,1)}, bf16[4,9,16,512]{3,2,1,0:T(8,128)(2,1)}, u32[]{:S(2)}, u32[]{:S(2)}) collective-permute-start(bf16[4,9,16,512]{3,2,1,0:T(8,128)(2,1)} %get-tuple-element.111), channel_id=1, source_target_pairs={{0,16},{4,20},{8,24},{12,28},{16,0},{20,4},{24,8},{28,12},{1,17},{... | collective-permute-start | bytes 1769480 | tf_op jit(solution)/shard_map/ppermute | solution.py:723
  218.2 48.2 %collective-permute-start.49 = (bf16[4,9,16,512]{3,2,1,0:T(8,128)(2,1)}, bf16[4,9,16,512]{3,2,1,0:T(8,128)(2,1)}, u32[]{:S(2)}, u32[]{:S(2)}) collective-permute-start(bf16[4,9,16,512]{3,2,1,0:T(8,128)(2,1)} %get-tuple-element.112), channel_id=1, source_target_pairs={{0,24},{4,28},{8,16},{12,20},{16,8},{20,12},{24,0},{28,4},{1,25},{... | collective-permute-start | bytes 1769480 | tf_op jit(solution)/shard_map/ppermute | solution.py:723
  220.3 6.4 %collective-permute-start.27 = (bf16[128,384]{1,0:T(8,128)(2,1)S(1)}, bf16[128,384]{1,0:T(8,128)(2,1)S(1)}, u32[]{:S(2)}, u32[]{:S(2)}) collective-permute-start(bf16[128,384]{1,0:T(8,128)(2,1)S(1)} %get-tuple-element.81), channel_id=1, source_target_pairs={{0,2},{1,3},{2,0},{3,1},{4,6},{5,7},{6,4},{7,5},{8,10},{9,11},{10,... | collective-permute-start | bytes 294920 | tf_op jit(solution)/shard_map/ppermute | solution.py:727
  227.3 4.6 %collective-permute-start.28 = (bf16[128,384]{1,0:T(8,128)(2,1)S(1)}, bf16[128,384]{1,0:T(8,128)(2,1)S(1)}, u32[]{:S(2)}, u32[]{:S(2)}) collective-permute-start(bf16[128,384]{1,0:T(8,128)(2,1)S(1)} %get-tuple-element.82), channel_id=1, source_target_pairs={{0,3},{1,0},{2,1},{3,2},{4,7},{5,4},{6,5},{7,6},{8,11},{9,8},{10,9... | collective-permute-start | bytes 294920 | tf_op jit(solution)/shard_map/ppermute | solution.py:727
  232.6 26.7 %collective-permute-start.34 = (bf16[4,9,16,256]{3,2,1,0:T(8,128)(2,1)}, bf16[4,9,16,256]{3,2,1,0:T(8,128)(2,1)}, u32[]{:S(2)}, u32[]{:S(2)}) collective-permute-start(bf16[4,9,16,256]{3,2,1,0:T(8,128)(2,1)} %get-tuple-element.98), channel_id=1, source_target_pairs={{0,16},{4,20},{8,24},{12,28},{16,0},{20,4},{24,8},{28,12},{1,17},{... | collective-permute-start | bytes 884744 | tf_op jit(solution)/shard_map/ppermute | solution.py:723
  233.8 25.5 %collective-permute-start.35 = (bf16[4,9,16,256]{3,2,1,0:T(8,128)(2,1)}, bf16[4,9,16,256]{3,2,1,0:T(8,128)(2,1)}, u32[]{:S(2)}, u32[]{:S(2)}) collective-permute-start(bf16[4,9,16,256]{3,2,1,0:T(8,128)(2,1)} %get-tuple-element.99), channel_id=1, source_target_pairs={{0,24},{4,28},{8,16},{12,20},{16,8},{20,12},{24,0},{28,4},{1,25},{... | collective-permute-start | bytes 884744 | tf_op jit(solution)/shard_map/ppermute | solution.py:723
  262.5 12.7 %collective-permute-start.36 = (bf16[9,16,256]{2,1,0:T(8,128)(2,1)S(1)}, bf16[9,16,256]{2,1,0:T(8,128)(2,1)S(1)}, u32[]{:S(2)}, u32[]{:S(2)}) collective-permute-start(bf16[9,16,256]{2,1,0:T(8,128)(2,1)S(1)} %get-tuple-element.101), channel_id=1, source_target_pairs={{0,1},{1,2},{2,3},{3,0},{4,5},{5,6},{6,7},{7,4},{8,9},{9,10},{10,1... | collective-permute-start | bytes 221192 | tf_op jit(solution)/shard_map/ppermute | solution.py:727
  262.6 15.0 %collective-permute-start.37 = (bf16[9,16,256]{2,1,0:T(8,128)(2,1)S(1)}, bf16[9,16,256]{2,1,0:T(8,128)(2,1)S(1)}, u32[]{:S(2)}, u32[]{:S(2)}) collective-permute-start(bf16[9,16,256]{2,1,0:T(8,128)(2,1)S(1)} %get-tuple-element.102), channel_id=1, source_target_pairs={{0,2},{1,3},{2,0},{3,1},{4,6},{5,7},{6,4},{7,5},{8,10},{9,11},{10,... | collective-permute-start | bytes 221192 | tf_op jit(solution)/shard_map/ppermute | solution.py:727
  265.4 13.3 %collective-permute-start.38 = (bf16[9,16,256]{2,1,0:T(8,128)(2,1)S(1)}, bf16[9,16,256]{2,1,0:T(8,128)(2,1)S(1)}, u32[]{:S(2)}, u32[]{:S(2)}) collective-permute-start(bf16[9,16,256]{2,1,0:T(8,128)(2,1)S(1)} %get-tuple-element.103), channel_id=1, source_target_pairs={{0,3},{1,0},{2,1},{3,2},{4,7},{5,4},{6,5},{7,6},{8,11},{9,8},{10,9... | collective-permute-start | bytes 221192 | tf_op jit(solution)/shard_map/ppermute | solution.py:727
  268.0 12.1 %collective-permute-start.50 = (bf16[9,16,512]{2,1,0:T(8,128)(2,1)S(1)}, bf16[9,16,512]{2,1,0:T(8,128)(2,1)S(1)}, u32[]{:S(2)}, u32[]{:S(2)}) collective-permute-start(bf16[9,16,512]{2,1,0:T(8,128)(2,1)S(1)} %get-tuple-element.114), channel_id=1, source_target_pairs={{0,1},{1,2},{2,3},{3,0},{4,5},{5,6},{6,7},{7,4},{8,9},{9,10},{10,1... | collective-permute-start | bytes 442376 | tf_op jit(solution)/shard_map/ppermute | solution.py:727
  269.2 20.8 %collective-permute-start.51 = (bf16[9,16,512]{2,1,0:T(8,128)(2,1)S(1)}, bf16[9,16,512]{2,1,0:T(8,128)(2,1)S(1)}, u32[]{:S(2)}, u32[]{:S(2)}) collective-permute-start(bf16[9,16,512]{2,1,0:T(8,128)(2,1)S(1)} %get-tuple-element.115), channel_id=1, source_target_pairs={{0,2},{1,3},{2,0},{3,1},{4,6},{5,7},{6,4},{7,5},{8,10},{9,11},{10,... | collective-permute-start | bytes 442376 | tf_op jit(solution)/shard_map/ppermute | solution.py:727
  275.2 26.4 %collective-permute-start.29 = (bf16[64,1536]{1,0:T(8,128)(2,1)S(1)}, bf16[64,1536]{1,0:T(8,128)(2,1)S(1)}, u32[]{:S(2)}, u32[]{:S(2)}) collective-permute-start(bf16[64,1536]{1,0:T(8,128)(2,1)S(1)} %get-tuple-element.91), channel_id=1, source_target_pairs={{0,1},{1,2},{2,3},{3,0},{4,5},{5,6},{6,7},{7,4},{8,9},{9,10},{10,1... | collective-permute-start | bytes 589832 | tf_op jit(solution)/shard_map/ppermute | solution.py:727
  277.6 26.1 %collective-permute-start.30 = (bf16[64,1536]{1,0:T(8,128)(2,1)S(1)}, bf16[64,1536]{1,0:T(8,128)(2,1)S(1)}, u32[]{:S(2)}, u32[]{:S(2)}) collective-permute-start(bf16[64,1536]{1,0:T(8,128)(2,1)S(1)} %get-tuple-element.92), channel_id=1, source_target_pairs={{0,2},{1,3},{2,0},{3,1},{4,6},{5,7},{6,4},{7,5},{8,10},{9,11},{10,... | collective-permute-start | bytes 589832 | tf_op jit(solution)/shard_map/ppermute | solution.py:727
  278.7 26.4 %collective-permute-start.31 = (bf16[64,1536]{1,0:T(8,128)(2,1)S(1)}, bf16[64,1536]{1,0:T(8,128)(2,1)S(1)}, u32[]{:S(2)}, u32[]{:S(2)}) collective-permute-start(bf16[64,1536]{1,0:T(8,128)(2,1)S(1)} %get-tuple-element.93), channel_id=1, source_target_pairs={{0,3},{1,0},{2,1},{3,2},{4,7},{5,4},{6,5},{7,6},{8,11},{9,8},{10,9... | collective-permute-start | bytes 589832 | tf_op jit(solution)/shard_map/ppermute | solution.py:727
  280.1 25.2 %collective-permute-start.44 = (bf16[9,16,256]{2,1,0:T(8,128)(2,1)S(1)}, bf16[9,16,256]{2,1,0:T(8,128)(2,1)S(1)}, u32[]{:S(2)}, u32[]{:S(2)}) collective-permute-start(bf16[9,16,256]{2,1,0:T(8,128)(2,1)S(1)} %in_chan_sum.1.rest_0_), channel_id=1, source_target_pairs={{0,24},{4,28},{8,16},{12,20},{16,8},{20,12},{24,0},{28,4},{1,25},{... | collective-permute-start | bytes 221192 | tf_op jit(solution)/shard_map/ppermute | solution.py:723
  290.1 11.4 %collective-permute-start.52 = (bf16[9,16,512]{2,1,0:T(8,128)(2,1)S(1)}, bf16[9,16,512]{2,1,0:T(8,128)(2,1)S(1)}, u32[]{:S(2)}, u32[]{:S(2)}) collective-permute-start(bf16[9,16,512]{2,1,0:T(8,128)(2,1)S(1)} %get-tuple-element.116), channel_id=1, source_target_pairs={{0,3},{1,0},{2,1},{3,2},{4,7},{5,4},{6,5},{7,6},{8,11},{9,8},{10,9... | collective-permute-start | bytes 442376 | tf_op jit(solution)/shard_map/ppermute | solution.py:727
  301.5 6.2 %collective-permute-start.42 = (bf16[9,16,256]{2,1,0:T(8,128)(2,1)S(1)}, bf16[9,16,256]{2,1,0:T(8,128)(2,1)S(1)}, u32[]{:S(2)}, u32[]{:S(2)}) collective-permute-start(bf16[9,16,256]{2,1,0:T(8,128)(2,1)S(1)} %in_chan_sum.1.rest_0_), channel_id=1, source_target_pairs={{0,16},{4,20},{8,24},{12,28},{16,0},{20,4},{24,8},{28,12},{1,17},{... | collective-permute-start | bytes 221192 | tf_op jit(solution)/shard_map/ppermute | solution.py:723
  301.6 6.1 %collective-permute-start.40 = (bf16[9,16,256]{2,1,0:T(8,128)(2,1)S(1)}, bf16[9,16,256]{2,1,0:T(8,128)(2,1)S(1)}, u32[]{:S(2)}, u32[]{:S(2)}) collective-permute-start(bf16[9,16,256]{2,1,0:T(8,128)(2,1)S(1)} %in_chan_sum.1.rest_0_), channel_id=1, source_target_pairs={{0,8},{4,12},{8,0},{12,4},{16,24},{20,28},{24,16},{28,20},{1,9},{5... | collective-permute-start | bytes 221192 | tf_op jit(solution)/shard_map/ppermute | solution.py:723
  303.7 7.7 %collective-permute-start.58 = (bf16[9,16,512]{2,1,0:T(8,128)(2,1)S(1)}, bf16[9,16,512]{2,1,0:T(8,128)(2,1)S(1)}, u32[]{:S(2)}, u32[]{:S(2)}) collective-permute-start(bf16[9,16,512]{2,1,0:T(8,128)(2,1)S(1)} %mid_chan_sum.1.rest_0_), channel_id=1, source_target_pairs={{0,24},{4,28},{8,16},{12,20},{16,8},{20,12},{24,0},{28,4},{1,25},{... | collective-permute-start | bytes 442376 | tf_op jit(solution)/shard_map/ppermute | solution.py:723
  305.1 8.0 %collective-permute-start.56 = (bf16[9,16,512]{2,1,0:T(8,128)(2,1)S(1)}, bf16[9,16,512]{2,1,0:T(8,128)(2,1)S(1)}, u32[]{:S(2)}, u32[]{:S(2)}) collective-permute-start(bf16[9,16,512]{2,1,0:T(8,128)(2,1)S(1)} %mid_chan_sum.1.rest_0_), channel_id=1, source_target_pairs={{0,16},{4,20},{8,24},{12,28},{16,0},{20,4},{24,8},{28,12},{1,17},{... | collective-permute-start | bytes 442376 | tf_op jit(solution)/shard_map/ppermute | solution.py:723
  305.3 7.9 %collective-permute-start.54 = (bf16[9,16,512]{2,1,0:T(8,128)(2,1)S(1)}, bf16[9,16,512]{2,1,0:T(8,128)(2,1)S(1)}, u32[]{:S(2)}, u32[]{:S(2)}) collective-permute-start(bf16[9,16,512]{2,1,0:T(8,128)(2,1)S(1)} %mid_chan_sum.1.rest_0_), channel_id=1, source_target_pairs={{0,8},{4,12},{8,0},{12,4},{16,24},{20,28},{24,16},{28,20},{1,9},{5... | collective-permute-start | bytes 442376 | tf_op jit(solution)/shard_map/ppermute | solution.py:723
  307.7 1.3 collective-permute-start.39
  307.7 1.4 collective-permute-start.45
  309.0 5.5 %collective-permute-start.43 = (bf16[9,16,256]{2,1,0:T(8,128)(2,1)S(1)}, bf16[9,16,256]{2,1,0:T(8,128)(2,1)S(1)}, u32[]{:S(2)}, u32[]{:S(2)}) collective-permute-start(bf16[9,16,256]{2,1,0:T(8,128)(2,1)S(1)} %collective-permute-done.42.rest_4_), channel_id=1, source_target_pairs={{0,4},{4,0},{8,12},{12,8},{16,20},{20,16},{24,28},{28,24},{1,5},{5... | collective-permute-start | bytes 221192 | tf_op jit(solution)/shard_map/ppermute | solution.py:723
  309.2 9.4 %collective-permute-start.53 = (bf16[9,16,512]{2,1,0:T(8,128)(2,1)S(1)}, bf16[9,16,512]{2,1,0:T(8,128)(2,1)S(1)}, u32[]{:S(2)}, u32[]{:S(2)}) collective-permute-start(bf16[9,16,512]{2,1,0:T(8,128)(2,1)S(1)} %mid_chan_sum.1.rest_0_), channel_id=1, source_target_pairs={{0,4},{4,0},{8,12},{12,8},{16,20},{20,16},{24,28},{28,24},{1,5},{5... | collective-permute-start | bytes 442376 | tf_op jit(solution)/shard_map/ppermute | solution.py:723
  311.4 7.1 %collective-permute-start.59 = (bf16[9,16,512]{2,1,0:T(8,128)(2,1)S(1)}, bf16[9,16,512]{2,1,0:T(8,128)(2,1)S(1)}, u32[]{:S(2)}, u32[]{:S(2)}) collective-permute-start(bf16[9,16,512]{2,1,0:T(8,128)(2,1)S(1)} %collective-permute-done.58.rest_6_), channel_id=1, source_target_pairs={{0,4},{4,0},{8,12},{12,8},{16,20},{20,16},{24,28},{28,24},{1,5},{5... | collective-permute-start | bytes 442376 | tf_op jit(solution)/shard_map/ppermute | solution.py:723
  313.1 5.4 %collective-permute-start.57 = (bf16[9,16,512]{2,1,0:T(8,128)(2,1)S(1)}, bf16[9,16,512]{2,1,0:T(8,128)(2,1)S(1)}, u32[]{:S(2)}, u32[]{:S(2)}) collective-permute-start(bf16[9,16,512]{2,1,0:T(8,128)(2,1)S(1)} %collective-permute-done.56.rest_4_), channel_id=1, source_target_pairs={{0,4},{4,0},{8,12},{12,8},{16,20},{20,16},{24,28},{28,24},{1,5},{5... | collective-permute-start | bytes 442376 | tf_op jit(solution)/shard_map/ppermute | solution.py:723
  313.1 5.4 %collective-permute-start.55 = (bf16[9,16,512]{2,1,0:T(8,128)(2,1)S(1)}, bf16[9,16,512]{2,1,0:T(8,128)(2,1)S(1)}, u32[]{:S(2)}, u32[]{:S(2)}) collective-permute-start(bf16[9,16,512]{2,1,0:T(8,128)(2,1)S(1)} %collective-permute-done.54.rest_2_), channel_id=1, source_target_pairs={{0,4},{4,0},{8,12},{12,8},{16,20},{20,16},{24,28},{28,24},{1,5},{5... | collective-permute-start | bytes 442376 | tf_op jit(solution)/shard_map/ppermute | solution.py:723
  314.5 2.4 collective-permute-start.41
  (50 other events, 476.4 us)
